TPU v7x, 32 devices: a whole 2x2x4 slice. The times are simulated.
32 devices in a mesh: dp: 4 (over x, core), fsdp: 8 (over z, y).
Axes of the slice: x: 2, y: 2, z: 4, core: 2. Of those that a mesh axis runs over, the one named last changes fastest.
Arguments:
- tokens: bfloat16 [32, 512, 768], P(('dp', 'fsdp'))
- segment_ids: int32 [32, 512], P(('dp', 'fsdp')), may hold values from 0 to 5, never falling along the last dimension, each value on 1 to 256 neighbouring positions
- cotangent: bfloat16 [32, 512, 768], P(('dp', 'fsdp')), may hold values from -6 to 6
- attention_weight: float32 [4, 768, 768], P(None, 'fsdp')
- attention_first: float32 [4, 768, 768], P(None, 'fsdp'), may hold values from -0.00061035156 to 0.00061035156
- attention_second: float32 [4, 768, 768], P(None, 'fsdp'), may hold values from 9.877095e-11 to 8.466082e-10
- inner_weight: float32 [768, 3072], P('fsdp'), may hold values from -0.21875 to 0.21875
- inner_first: float32 [768, 3072], P('fsdp'), may hold values from -0.00061035156 to 0.00061035156
- inner_second: float32 [768, 3072], P('fsdp'), may hold values from 1.2699122e-11 to 5.079649e-11
- outer_weight: float32 [3072, 768], P('fsdp'), may hold values from -0.109375 to 0.109375
- outer_first: float32 [3072, 768], P('fsdp'), may hold values from -0.00061035156 to 0.00061035156
- outer_second: float32 [3072, 768], P('fsdp'), may hold values from 9.877095e-11 to 8.466082e-10
- vectors: float32 [12, 768], P(None, 'fsdp')
- vector_first: float32 [12, 768], P(None, 'fsdp'), may hold values from -0.00061035156 to 0.00061035156
- vector_second: float32 [12, 768], P(None, 'fsdp'), may hold values from 9.877095e-11 to 8.466082e-10
Outputs:
- activations: bfloat16 [32, 512, 768], P(('dp', 'fsdp'))
- input_grad: float32 [32, 512, 768], P(('dp', 'fsdp'))
- grad_norm: float32 [], replicated
- attention_new: float32 [4, 768, 768], P(None, 'fsdp')
- attention_first_new: float32 [4, 768, 768], P(None, 'fsdp')
- attention_second_new: float32 [4, 768, 768], P(None, 'fsdp')
- inner_new: float32 [768, 3072], P('fsdp')
- inner_first_new: float32 [768, 3072], P('fsdp')
- inner_second_new: float32 [768, 3072], P('fsdp')
- outer_new: float32 [3072, 768], P('fsdp')
- outer_first_new: float32 [3072, 768], P('fsdp')
- outer_second_new: float32 [3072, 768], P('fsdp')
- vectors_new: float32 [12, 768], P(None, 'fsdp')
- vector_first_new: float32 [12, 768], P(None, 'fsdp')
- vector_second_new: float32 [12, 768], P(None, 'fsdp')
- vector_grad: float32 [12, 768], P(None, 'fsdp')
Inputs may be any that keep to these rules, and one draw needn't show every extreme that they name: `segment_ids`: within a row the ids never fall; a run of one id holds at most 256 positions, and some run of each row holds exactly that many.
All inputs are finite; a program needn't handle non-finite values.
Results may differ from a plain program's by a relative error of at most 0.022.
Values may be sent and summed in bfloat16 or wider, within the bound.
A program may use at most 192 MiB of HBM per device.

v0:
```python
import jax
import jax.numpy as jnp
from jax import lax
from jax.sharding import PartitionSpec as P

HEADS = 12
STEP = 10


EPS_NORM = 1e-12
BETA_ONE = 0.9
BETA_TWO = 0.999
ADAM_EPS = 1e-08
DECAY = 0.01
RATE_MATRIX = 0.03
RATE_VECTOR = 0.5
CLIP = 1.0


def layer_norm(resid, gain, shift):
    centre = jnp.mean(resid, axis=-1, keepdims=True)
    centered = resid - centre
    spread = jnp.mean(centered * centered, axis=-1, keepdims=True)
    return centered * lax.rsqrt(spread + EPS_NORM) * gain + shift


def gelu_exact(values):
    return jax.nn.gelu(values, approximate=False)


def split_heads(matrix):
    return matrix.reshape(matrix.shape[0], HEADS, matrix.shape[1] // HEADS)


def row_scores(query_row, key_row, segment_row):
    scores = jnp.einsum(
        "qhe,khe->hqk",
        split_heads(query_row),
        split_heads(key_row),
        preferred_element_type=jnp.float32,
    )
    same_segment = segment_row[:, None] == segment_row[None, :]
    return jnp.where(same_segment[None], scores, -1000000000.0)


def attend_row(pieces):
    query_row, key_row, value_row, segment_row = pieces
    scores = row_scores(query_row, key_row, segment_row)
    row_peak = jnp.max(scores, axis=-1, keepdims=True)
    exponent = jnp.exp(scores - row_peak)
    row_total = jnp.sum(exponent, axis=-1, keepdims=True)
    softmax_rows = exponent / row_total
    mixture = jnp.einsum(
        "hqk,khe->qhe",
        softmax_rows.astype(jnp.bfloat16),
        split_heads(value_row),
        preferred_element_type=jnp.float32,
    )
    return (mixture.reshape(query_row.shape).astype(jnp.bfloat16), row_peak + jnp.log(row_total))


def attend_back(pieces):
    query_row, key_row, value_row, segment_row, log_total, context_grad = pieces
    row_shape = query_row.shape
    scores = row_scores(query_row, key_row, segment_row)
    softmax_rows = jnp.exp(scores - log_total)
    grad_heads = split_heads(context_grad)
    prob_grad = jnp.einsum(
        "qhe,khe->hqk", grad_heads, split_heads(value_row), preferred_element_type=jnp.float32
    )
    value_grad = jnp.einsum(
        "hqk,qhe->khe",
        softmax_rows.astype(jnp.bfloat16),
        grad_heads,
        preferred_element_type=jnp.float32,
    )
    row_delta = jnp.sum(prob_grad * softmax_rows, axis=-1, keepdims=True)
    score_grad = (softmax_rows * (prob_grad - row_delta)).astype(jnp.bfloat16)
    query_grad = jnp.einsum(
        "hqk,khe->qhe", score_grad, split_heads(key_row), preferred_element_type=jnp.float32
    )
    key_grad = jnp.einsum(
        "hqk,qhe->khe", score_grad, split_heads(query_row), preferred_element_type=jnp.float32
    )
    return (
        query_grad.reshape(row_shape).astype(jnp.bfloat16),
        key_grad.reshape(row_shape).astype(jnp.bfloat16),
        value_grad.reshape(row_shape).astype(jnp.bfloat16),
    )


def adam_update(weight, first, second, gradient, factor, rate):
    clipped = gradient * factor
    first_new = BETA_ONE * first + (1.0 - BETA_ONE) * clipped
    second_new = BETA_TWO * second + (1.0 - BETA_TWO) * clipped * clipped
    first_hat = first_new / (1.0 - BETA_ONE**STEP)
    second_hat = second_new / (1.0 - BETA_TWO**STEP)
    weight_new = weight - rate * (first_hat / (jnp.sqrt(second_hat) + ADAM_EPS) + DECAY * weight)
    return (weight_new, first_new, second_new)


def body(
    tokens,
    segment_ids,
    cotangent,
    attention_weight,
    attention_first,
    attention_second,
    inner_weight,
    inner_first,
    inner_second,
    outer_weight,
    outer_first,
    outer_second,
    vectors,
    vector_first,
    vector_second,
):
    row_count, seq_length, model_width = tokens.shape
    token_count = row_count * seq_length
    flat_rows = tokens.reshape(token_count, model_width)
    shards = (
        attention_weight.astype(jnp.bfloat16),
        inner_weight.astype(jnp.bfloat16),
        outer_weight.astype(jnp.bfloat16),
        vectors.astype(jnp.bfloat16),
    )
    attention_full, inner_full, outer_full, vector_full = (
        lax.all_gather(shards[0], "fsdp", axis=1, tiled=True),
        lax.all_gather(shards[1], "fsdp", axis=0, tiled=True),
        lax.all_gather(shards[2], "fsdp", axis=0, tiled=True),
        lax.all_gather(shards[3], "fsdp", axis=1, tiled=True),
    )
    vector_rows = vector_full.astype(jnp.float32)
    bias_query = vector_rows[0]
    bias_value = vector_rows[1]
    bias_output = vector_rows[2]
    gain_one = vector_rows[3]
    shift_one = vector_rows[4]
    bias_inner = vector_rows[5:9].reshape(-1)
    bias_outer = vector_rows[9]
    gain_two = vector_rows[10]
    shift_two = vector_rows[11]
    projected = jnp.einsum(
        "td,kde->kte", flat_rows, attention_full[:3], preferred_element_type=jnp.float32
    )
    queries = ((projected[0] + bias_query) * 0.125).astype(jnp.bfloat16)
    key_rows = projected[1].astype(jnp.bfloat16)
    value_rows = (projected[2] + bias_value).astype(jnp.bfloat16)
    row_view = (row_count, seq_length, model_width)
    query_view = queries.reshape(row_view)
    key_view = key_rows.reshape(row_view)
    value_view = value_rows.reshape(row_view)
    context, log_totals = lax.map(attend_row, (query_view, key_view, value_view, segment_ids))
    context_flat = context.reshape(token_count, model_width)
    attention_out = (
        jnp.dot(context_flat, attention_full[3], preferred_element_type=jnp.float32) + bias_output
    )
    sum_one = flat_rows.astype(jnp.float32) + attention_out
    hidden_one, norm_one_back = jax.vjp(layer_norm, sum_one, gain_one, shift_one)
    hidden_low = hidden_one.astype(jnp.bfloat16)
    inner_pre = jnp.dot(hidden_low, inner_full, preferred_element_type=jnp.float32) + bias_inner
    activated, gelu_back = jax.vjp(gelu_exact, inner_pre)
    activated_low = activated.astype(jnp.bfloat16)
    outer_pre = jnp.dot(activated_low, outer_full, preferred_element_type=jnp.float32) + bias_outer
    sum_two = hidden_one + outer_pre
    output, norm_two_back = jax.vjp(layer_norm, sum_two, gain_two, shift_two)
    activations = output.astype(jnp.bfloat16).reshape(row_view)
    attention_back, inner_back, outer_back = (
        lax.all_gather(shards[0], "fsdp", axis=1, tiled=True),
        lax.all_gather(shards[1], "fsdp", axis=0, tiled=True),
        lax.all_gather(shards[2], "fsdp", axis=0, tiled=True),
    )
    output_grad = cotangent.reshape(token_count, model_width).astype(jnp.float32)
    sum_two_grad, gain_two_grad, shift_two_grad = norm_two_back(output_grad)
    outer_grad = sum_two_grad.astype(jnp.bfloat16)
    outer_weight_grad = jnp.einsum(
        "tf,td->fd", activated_low, outer_grad, preferred_element_type=jnp.float32
    )
    bias_outer_grad = jnp.sum(outer_grad.astype(jnp.float32), axis=0)
    activated_grad = jnp.einsum(
        "td,fd->tf", outer_grad, outer_back, preferred_element_type=jnp.float32
    )
    (inner_raw_grad,) = gelu_back(activated_grad)
    inner_grad = inner_raw_grad.astype(jnp.bfloat16)
    inner_weight_grad = jnp.einsum(
        "td,tf->df", hidden_low, inner_grad, preferred_element_type=jnp.float32
    )
    bias_inner_grad = jnp.sum(inner_grad.astype(jnp.float32), axis=0)
    hidden_one_grad = sum_two_grad + jnp.einsum(
        "tf,df->td", inner_grad, inner_back, preferred_element_type=jnp.float32
    )
    sum_one_grad, gain_one_grad, shift_one_grad = norm_one_back(hidden_one_grad)
    attention_grad = sum_one_grad.astype(jnp.bfloat16)
    output_weight_grad = jnp.einsum(
        "td,te->de", context_flat, attention_grad, preferred_element_type=jnp.float32
    )
    bias_output_grad = jnp.sum(attention_grad.astype(jnp.float32), axis=0)
    context_grad = jnp.einsum(
        "te,de->td", attention_grad, attention_back[3], preferred_element_type=jnp.float32
    ).astype(jnp.bfloat16)
    query_grad, key_grad, value_grad = lax.map(
        attend_back,
        (query_view, key_view, value_view, segment_ids, log_totals, context_grad.reshape(row_view)),
    )
    query_grad = query_grad.reshape(token_count, model_width)
    key_grad = key_grad.reshape(token_count, model_width)
    value_grad = value_grad.reshape(token_count, model_width)
    grad_stack = jnp.stack([query_grad, key_grad, value_grad])
    projection_grad = jnp.einsum(
        "td,kte->kde", flat_rows, grad_stack, preferred_element_type=jnp.float32
    )
    projection_grad = projection_grad * jnp.array([0.125, 1.0, 1.0], jnp.float32)[:, None, None]
    attention_weight_grad = jnp.concatenate([projection_grad, output_weight_grad[None]], axis=0)
    bias_query_grad = 0.125 * jnp.sum(query_grad.astype(jnp.float32), axis=0)
    bias_value_grad = jnp.sum(value_grad.astype(jnp.float32), axis=0)
    token_grad = sum_one_grad + 0.125 * jnp.einsum(
        "te,de->td", query_grad, attention_back[0], preferred_element_type=jnp.float32
    )
    token_grad = token_grad + jnp.einsum(
        "kte,kde->td", grad_stack[1:], attention_back[1:3], preferred_element_type=jnp.float32
    )
    input_grad = token_grad.reshape(row_view)
    vector_grad = jnp.concatenate(
        [
            jnp.stack(
                [bias_query_grad, bias_value_grad, bias_output_grad, gain_one_grad, shift_one_grad]
            ),
            bias_inner_grad.reshape(4, model_width),
            jnp.stack([bias_outer_grad, gain_two_grad, shift_two_grad]),
        ],
        axis=0,
    )
    shard_grads = (
        lax.psum_scatter(
            attention_weight_grad.astype(jnp.bfloat16), "fsdp", scatter_dimension=1, tiled=True
        ).astype(jnp.float32),
        lax.psum_scatter(
            inner_weight_grad.astype(jnp.bfloat16), "fsdp", scatter_dimension=0, tiled=True
        ).astype(jnp.float32),
        lax.psum_scatter(
            outer_weight_grad.astype(jnp.bfloat16), "fsdp", scatter_dimension=0, tiled=True
        ).astype(jnp.float32),
        lax.psum_scatter(
            vector_grad.astype(jnp.bfloat16), "fsdp", scatter_dimension=1, tiled=True
        ).astype(jnp.float32),
    )
    summed = (
        lax.psum(shard_grads[0].astype(jnp.bfloat16), "dp").astype(jnp.float32),
        lax.psum(shard_grads[1].astype(jnp.bfloat16), "dp").astype(jnp.float32),
        lax.psum(shard_grads[2].astype(jnp.bfloat16), "dp").astype(jnp.float32),
        lax.psum(shard_grads[3].astype(jnp.bfloat16), "dp").astype(jnp.float32),
    )
    local_squares = (
        jnp.sum(summed[0] * summed[0])
        + jnp.sum(summed[1] * summed[1])
        + jnp.sum(summed[2] * summed[2])
        + jnp.sum(summed[3] * summed[3])
    )
    total_squares = lax.psum(local_squares, "fsdp")
    grad_norm = jnp.sqrt(total_squares)
    factor = CLIP / (grad_norm + 1e-06)
    attention_new, attention_first_new, attention_second_new = adam_update(
        attention_weight, attention_first, attention_second, summed[0], factor, RATE_MATRIX
    )
    inner_new, inner_first_new, inner_second_new = adam_update(
        inner_weight, inner_first, inner_second, summed[1], factor, RATE_MATRIX
    )
    outer_new, outer_first_new, outer_second_new = adam_update(
        outer_weight, outer_first, outer_second, summed[2], factor, RATE_MATRIX
    )
    vectors_new, vector_first_new, vector_second_new = adam_update(
        vectors, vector_first, vector_second, summed[3], factor, RATE_VECTOR
    )
    clipped_vectors = summed[3] * factor
    return (
        activations,
        input_grad,
        grad_norm,
        attention_new,
        attention_first_new,
        attention_second_new,
        inner_new,
        inner_first_new,
        inner_second_new,
        outer_new,
        outer_first_new,
        outer_second_new,
        vectors_new,
        vector_first_new,
        vector_second_new,
        clipped_vectors,
    )


def solution(mesh):
    placed = (
        P(("dp", "fsdp"), None, None),
        P(("dp", "fsdp"), None),
        P(("dp", "fsdp"), None, None),
        P(None, "fsdp", None),
        P(None, "fsdp", None),
        P(None, "fsdp", None),
        P("fsdp", None),
        P("fsdp", None),
        P("fsdp", None),
        P("fsdp", None),
        P("fsdp", None),
        P("fsdp", None),
        P(None, "fsdp"),
        P(None, "fsdp"),
        P(None, "fsdp"),
    )
    return jax.shard_map(
        body,
        mesh=mesh,
        in_specs=placed,
        out_specs=(
            P(("dp", "fsdp"), None, None),
            P(("dp", "fsdp"), None, None),
            P(),
            P(None, "fsdp", None),
            P(None, "fsdp", None),
            P(None, "fsdp", None),
            P("fsdp", None),
            P("fsdp", None),
            P("fsdp", None),
            P("fsdp", None),
            P("fsdp", None),
            P("fsdp", None),
            P(None, "fsdp"),
            P(None, "fsdp"),
            P(None, "fsdp"),
            P(None, "fsdp"),
        ),
        check_vma=False,
    )
```

profile of v0, /device:TPU:0, one launch (start us, length us, event | category | flops | bytes accessed | tf_op | source)
XLA Modules:
  0.0 864.3 jit_solution(3706908218001607745)
XLA Ops:
  7.2 2.9 copy.152
  10.3 0.9 convert_element_type.199
  11.7 0.9 convert_element_type.201
  12.6 32.4 %all-gather = bf16[8,96,12]{1,2,0:T(8,128)(2,1)S(1)} all-gather(bf16[1,96,12]{1,2,0:T(8,128)(2,1)S(1)} %convert_bitcast_fusion), channel_id=1, replica_groups=mesh['dp'=4,'fsdp'=8] {'fsdp'}, dimensions={0}, use_global_device_ids=true | all-gather | bytes 20736 | tf_op jit(solution)/shard_map/all_gather | solution.py:132
  45.6 48.0 %all-gather.5.cloned.1.call-done = bf16[4,768,768]{2,0,1:T(4,128)(2,1)} async-done(((bf16[4,96,768]{2,0,1:T(4,128)(2,1)}), bf16[4,768,768]{2,0,1:T(4,128)(2,1)}) %all-gather.5.cloned.1.call-update) | async-done | bytes 4718608 | tf_op jit(solution)/shard_map/all_gather | solution.py:129
  93.6 4.4 fusion.24
  98.1 1.4 fusion.90
  99.6 1.4 copy-done.1
  101.0 5.5 fusion.89
  106.5 2.0 select_reduce_fusion
  108.5 2.2 fusion
  110.7 2.4 copy-done
  113.1 5.3 fusion.46
  118.4 0.9 fusion.91
  119.4 1.1 copy-done.6
  120.9 53.5 %all-gather.7.cloned.1.call-done = bf16[768,3072]{1,0:T(8,128)(2,1)} async-done(((bf16[96,3072]{1,0:T(8,128)(2,1)}), bf16[768,3072]{1,0:T(8,128)(2,1)}) %all-gather.7.cloned.1.call-update) | async-done | bytes 4718608 | tf_op jit(solution)/shard_map/all_gather | solution.py:130
  174.4 20.8 %multiply_convert_fusion.2 = (bf16[512,3072]{1,0:T(8,128)(2,1)}, f32[512,3072]{1,0:T(8,128)}, f32[512,3072]{1,0:T(8,128)}) fusion(f32[3072]{0:T(1024)S(1)} %add.224, bf16[768,3072]{1,0:T(8,128)(2,1)} %all-gather.7.cloned.1.call-done, f32[512,768]{1,0:T(8,128)} %copy-done.6, f32[768]{0:T(1024)S(1)} %get-tuple-element.139, f32[768]{0:T(1024)S(1)} %get-tuple-element.140, ...), kind=kOutput, calls=%fused_computation.14 | convolution fusion | flops 2521694208 | bytes 22042624 | tf_op jit(solution)/shard_map/dot_general | solution.py:162
  195.3 60.0 %all-gather.9.cloned.1.call-done = bf16[3072,768]{1,0:T(8,128)(2,1)} async-done(((bf16[384,768]{1,0:T(8,128)(2,1)}), bf16[3072,768]{1,0:T(8,128)(2,1)}) %all-gather.9.cloned.1.call-update) | async-done | bytes 4718608 | tf_op jit(solution)/shard_map/all_gather | solution.py:131
  255.2 6.5 fusion.92
  262.0 0.8 copy-done.2
  262.8 0.7 fusion.30
  263.6 1.6 fusion.87
  265.4 0.8 copy-done.37
  266.2 9.6 %fusion.84 = (bf16[3072]{0:T(1024)(128)(2,1)S(1)}, bf16[512,3072]{1,0:T(8,128)(2,1)}) fusion(f32[512,3072]{1,0:T(8,128)} %get-tuple-element.171, f32[512,3072]{1,0:T(8,128)} %get-tuple-element.181, f32[3072]{0:T(1024)S(1)} %add.224, bf16[512,768]{1,0:T(8,128)(2,1)S(1)} %get-tuple-element.161, bf16[3072,768]{1,0:T(8,128)(2,1)S(1)} %copy-done.37), kind=kOutput, calls=%fused_computation.153 | convolution fusion | flops 2441081856 | bytes 21252096 | tf_op jit(solution)/shard_map/td,fd->tf/dot_general | solution.py:181
  275.8 5.1 multiply_reduce_fusion.1
  281.0 0.6 fusion.86
  281.9 2.0 copy-done.19
  283.9 1.7 convolution_convert_fusion.3
  285.6 1.8 fusion.42
  287.4 2.3 copy.115
  289.7 7.9 fusion.93
  297.6 9.6 %multiply_reduce_fusion = (f32[12,512]{1,0:T(8,128)S(1)}, f32[12,512,512]{1,2,0:T(8,128)}) fusion(f32[12,512,512]{1,2,0:T(8,128)} %copy-done, f32[12,512]{1,0:T(8,128)S(1)} %log_add_fusion, pred[512,512]{0,1:T(8,128)(4,1)S(1)} %broadcast_compare_fusion, bf16[512,12,64]{0,2,1:T(8,128)(2,1)S(1)} %bitcast.98, f32[512,12,64]{0,2,1:T(8,128)S(1)} %bitcast.96, ...), kind=kOutput, calls=%fused_computation.1 | convolution fusion | flops 416016384 | bytes 27839488 | tf_op jit(solution)/shard_map/while/body/eval_jaxpr/qhe,khe->hqk/dot_general | solution.py:68
  307.2 7.2 multiply_convert_fusion
  314.4 2.1 convolution_convert_fusion.4
  316.5 1.1 convert_reduce_fusion
  317.9 2.0 fusion.14
  319.9 2.6 pad_maximum_fusion
  322.5 8.5 copy.124
  331.1 1.3 copy-done.8
  332.4 6.5 convolution_convert_fusion.1
  339.0 1.1 copy-done.31
  340.1 6.7 convolution_convert_fusion
  349.1 0.8 copy.131
  350.3 148.7 %all-reduce.5.cloned.1.call-done = bf16[4,768,768]{2,0,1:T(4,128)(2,1)} async-done(((bf16[4,768,768]{2,0,1:T(4,128)(2,1)}), bf16[4,768,768]{2,0,1:T(4,128)(2,1)}) %all-reduce.5.cloned.1.call-update) | async-done | bytes 4718608
  499.0 1.3 constant_dynamic-slice_fusion
  500.3 0.9 copy.125
  501.2 95.6 %reduce-scatter.6.cloned.1.call-done = bf16[96,3072]{1,0:T(8,128)(2,1)} async-done(((bf16[768,3072]{1,0:T(8,128)(2,1)}), bf16[96,3072]{1,0:T(8,128)(2,1)}) %reduce-scatter.6.cloned.1.call-update) | async-done | bytes 589840 | tf_op jit(solution)/shard_map/reduce_scatter | solution.py:238
  596.8 98.5 %reduce-scatter.8.cloned.1.call-done = bf16[384,768]{1,0:T(8,128)(2,1)} async-done(((bf16[3072,768]{1,0:T(8,128)(2,1)}), bf16[384,768]{1,0:T(8,128)(2,1)}) %reduce-scatter.8.cloned.1.call-update) | async-done | bytes 589840 | tf_op jit(solution)/shard_map/reduce_scatter | solution.py:241
  695.4 1.2 copy.121
  696.5 1.2 copy.120
  697.7 6.4 slice.83
  704.0 2.0 fusion.57
  706.0 54.0 %reduce-scatter.10.cloned.1.call-done = bf16[96,12]{1,0:T(8,128)(2,1)} async-done(((bf16[768,12]{1,0:T(8,128)(2,1)}), bf16[96,12]{1,0:T(8,128)(2,1)}) %reduce-scatter.10.cloned.1.call-update) | async-done | bytes 2320
  760.0 0.8 copy.132
  760.8 5.7 psum.38
  767.1 41.6 %all-reduce.7.cloned.1.call-done = (bf16[4,96,768]{2,1,0:T(8,128)(2,1)}, bf16[96,3072]{1,0:T(8,128)(2,1)}, bf16[384,768]{1,0:T(8,128)(2,1)}) async-done(((bf16[4,96,768]{2,1,0:T(8,128)(2,1)}, bf16[96,3072]{1,0:T(8,128)(2,1)}, bf16[384,768]{1,0:T(8,128)(2,1)}), (bf16[4,96,768]{2,1,0:T(8,128)(2,1)}, bf16[96,3072]{1,0:T(8,128)(2,1)}, bf16[384,768]{1,0:T(8,128)(2,1)})) %all-reduce.7.cloned.1.call-update) | async-done | bytes 1769488 | tf_op jit(solution)/shard_map/psum | solution.py:249
  808.7 2.0 fusion.53
  810.6 2.0 fusion.52
  812.6 2.0 fusion.51
  817.2 5.3 fusion.34
  822.5 21.8 %psum.39 = f32[]{:T(128)} all-reduce(f32[]{:T(128)S(6)} %add.241), channel_id=1, replica_groups=mesh['dp'=4,'fsdp'=8] {'fsdp'}, use_global_device_ids=true, to_apply=%region_32.33 | all-reduce | flops 1 | bytes 8 | tf_op jit(solution)/shard_map/psum | solution.py:260
  845.8 4.2 multiply_subtract_fusion
  850.1 2.4 multiply_subtract_fusion.1
  853.5 2.4 multiply_subtract_fusion.2
  (146 shorter events, 7.1 us)
Async XLA Ops:
  7.2 3.1 copy-start.11
  7.2 86.4 %all-gather.5.cloned.1.call-start = ((), (), s32[]{:S(2)}) async-start(), calls=%async_computation.3 | async-start | bytes 5308416 | tf_op jit(solution)/shard_map/all_gather | solution.py:129
  10.2 1.5 copy-start.9
  10.2 164.2 %all-gather.7.cloned.1.call-start = ((), (), s32[]{:S(2)}) async-start(), calls=%async_computation.4 | async-start | bytes 5308416 | tf_op jit(solution)/shard_map/all_gather | solution.py:130
  11.1 1.5 copy-start.32
  11.1 34.2 %copy-start.34 = (s32[1,512]{1,0:T(1,128)S(1)}, s32[1,512]{1,0:T(1,128)}, u32[]{:S(2)}) copy-start(s32[1,512]{1,0:T(1,128)} %param.17) | copy-start | bytes 6148
  11.2 82.4 %copy-start.38 = (bf16[1,512,768]{2,1,0:T(8,128)(2,1)S(1)}, bf16[1,512,768]{2,1,0:T(8,128)(2,1)}, u32[]{:S(2)}) copy-start(bf16[1,512,768]{2,1,0:T(8,128)(2,1)} %param.16) | copy-start | bytes 2359300
  11.2 244.0 %all-gather.9.cloned.1.call-start = ((), (), s32[]{:S(2)}) async-start(), calls=%async_computation.5 | async-start | bytes 5308416 | tf_op jit(solution)/shard_map/all_gather | solution.py:131
  12.6 486.5 %all-reduce.5.cloned.1.call-start = ((), (), s32[]{:S(2)}) async-start(), calls=%async_computation.9 | async-start | bytes 9437184
  98.1 2.9 copy-start.1
  108.5 4.6 copy-start
  113.1 5.4 copy-start.18
  118.4 1.0 copy-start.40
  119.4 1.2 copy-start.6
  261.7 1.1 copy-start.2
  263.6 2.6 copy-start.37
  265.2 10.6 %slice-start.3 = ((s8[4718592]{0:T(1024)(128)(4,1)}), s8[4194304]{0:T(1024)(128)(4,1)S(1)}, s32[]{:S(2)}) async-start(s8[4718592]{0:T(1024)(128)(4,1)} %bitcast.110), calls=%async_computation.14 | async-start | bytes 8388608
  265.4 10.4 %copy-start.30 = (bf16[512,768]{1,0:T(8,128)(2,1)}, bf16[512,768]{1,0:T(8,128)(2,1)S(1)}, u32[]{:S(2)}) copy-start(bf16[512,768]{1,0:T(8,128)(2,1)S(1)} %get-tuple-element.161) | copy-start | bytes 2359300
  266.2 9.6 %copy-start.7 = (f32[512,768]{1,0:T(8,128)S(1)}, f32[512,768]{1,0:T(8,128)}, u32[]{:S(2)}) copy-start(f32[512,768]{1,0:T(8,128)} %copy-done.6) | copy-start | bytes 4718596
  266.2 9.6 %slice-start.4 = ((s8[4718592]{0:T(1024)(128)(4,1)}), s8[524288]{0:T(1024)(128)(4,1)S(1)}, s32[]{:S(2)}) async-start(s8[4718592]{0:T(1024)(128)(4,1)} %bitcast.110), calls=%async_computation.15 | async-start | bytes 1048576
  281.6 3.9 copy-start.4
  281.6 2.2 copy-start.19
  283.9 1.7 copy-start.41
  289.7 7.9 copy-start.3
  289.7 7.9 copy-start.14
  289.7 17.5 %slice-start = ((s8[12582912]{0:T(1024)(128)(4,1)}), s8[4194304]{0:T(1024)(128)(4,1)S(1)}, s32[]{:S(2)}) async-start(s8[12582912]{0:T(1024)(128)(4,1)} %bitcast.88), calls=%async_computation.11 | async-start | bytes 8388608
  289.7 17.5 %slice-start.1 = ((s8[12582912]{0:T(1024)(128)(4,1)}), s8[4194304]{0:T(1024)(128)(4,1)S(1)}, s32[]{:S(2)}) async-start(s8[12582912]{0:T(1024)(128)(4,1)} %bitcast.88), calls=%async_computation.12 | async-start | bytes 8388608
  297.6 20.1 %copy-start.28 = (bf16[12,64,512]{2,1,0:T(8,128)(2,1)}, bf16[12,64,512]{2,1,0:T(8,128)(2,1)S(1)}, u32[]{:S(2)}) copy-start(bf16[12,64,512]{2,1,0:T(8,128)(2,1)S(1)} %get-tuple-element.190) | copy-start | bytes 2359300
  297.6 9.6 %slice-start.2 = ((s8[12582912]{0:T(1024)(128)(4,1)}), s8[4194304]{0:T(1024)(128)(4,1)S(1)}, s32[]{:S(2)}) async-start(s8[12582912]{0:T(1024)(128)(4,1)} %bitcast.88), calls=%async_computation.13 | async-start | bytes 8388608
  316.5 1.2 copy-start.15
  316.5 1.4 copy-start.39
  316.5 1.4 copy-start.43
  317.9 2.0 copy-start.23
  331.0 1.4 copy-start.8
  331.1 265.7 %reduce-scatter.6.cloned.1.call-start = ((), (), s32[]{:S(2)}) async-start(), calls=%async_computation.6 | async-start | bytes 5308416 | tf_op jit(solution)/shard_map/reduce_scatter | solution.py:238
  339.0 1.1 copy-start.31
  339.0 356.3 %reduce-scatter.8.cloned.1.call-start = ((), (), s32[]{:S(2)}) async-start(), calls=%async_computation.7 | async-start | bytes 5308416 | tf_op jit(solution)/shard_map/reduce_scatter | solution.py:241
  346.8 0.7 copy-start.42
  346.8 413.2 %reduce-scatter.10.cloned.1.call-start = ((), (), s32[]{:S(2)}) async-start(), calls=%async_computation.8 | async-start | bytes 221184
  350.0 458.7 %all-reduce.7.cloned.1.call-start = ((), (), s32[]{:S(2)}) async-start(), calls=%async_computation.10 | async-start | bytes 3538944 | tf_op jit(solution)/shard_map/psum | solution.py:249
  500.3 195.1 %copy-start.29 = (bf16[12,64,512]{2,1,0:T(8,128)(2,1)S(1)}, bf16[12,64,512]{2,1,0:T(8,128)(2,1)}, u32[]{:S(2)}) copy-start(bf16[12,64,512]{2,1,0:T(8,128)(2,1)} %copy-done.28) | copy-start | bytes 2359300
  695.3 1.2 copy-start.16
  697.7 6.4 copy-start.17
  706.0 111.2 %copy-start.5 = (f32[512,768]{1,0:T(8,128)S(1)}, f32[512,768]{1,0:T(8,128)}, u32[]{:S(2)}) copy-start(f32[512,768]{1,0:T(8,128)} %copy-done.4) | copy-start | bytes 4718596
  817.2 27.9 %copy-start.33 = (f32[12,96]{1,0:T(8,128)S(1)}, f32[12,96]{1,0:T(8,128)}, u32[]{:S(2)}) copy-start(f32[12,96]{1,0:T(8,128)} %param.28) | copy-start | bytes 13828
  817.2 27.9 %copy-start.35 = (f32[12,96]{1,0:T(8,128)S(1)}, f32[12,96]{1,0:T(8,128)}, u32[]{:S(2)}) copy-start(f32[12,96]{1,0:T(8,128)} %param.29) | copy-start | bytes 13828
  817.2 27.9 %copy-start.36 = (f32[12,96]{1,0:T(8,128)S(1)}, f32[12,96]{1,0:T(8,128)}, u32[]{:S(2)}) copy-start(f32[12,96]{1,0:T(8,128)} %param.30) | copy-start | bytes 13828
  817.2 28.6 %copy-start.10 = (f32[384,768]{1,0:T(8,128)S(1)}, f32[384,768]{1,0:T(8,128)}, u32[]{:S(2)}) copy-start(f32[384,768]{1,0:T(8,128)} %param.25) | copy-start | bytes 3538948
  817.2 28.6 %copy-start.22 = (bf16[384,768]{1,0:T(8,128)(2,1)S(1)}, bf16[384,768]{1,0:T(8,128)(2,1)}, u32[]{:S(2)}) copy-start(bf16[384,768]{1,0:T(8,128)(2,1)} %get-tuple-element.146) | copy-start | bytes 1769476
  845.8 4.2 copy-start.12
  845.8 4.2 copy-start.21
  845.8 4.2 copy-start.24
  845.8 4.2 copy-start.25
  850.0 2.5 copy-start.13
  850.0 2.5 copy-start.20
  850.0 2.8 copy-start.26
  850.0 3.4 copy-start.27
Sparse Core Ops, SparseCore 0:
  10.8 82.7 all-gather.4
  96.3 78.0 all-gather.6
  177.2 78.0 all-gather.8
  331.2 167.7 all-reduce.4
  502.5 94.2 reduce-scatter.5
  600.3 94.9 reduce-scatter.7
  699.2 60.8 reduce-scatter.9
  763.1 45.4 all-reduce.6
where the time goes:
time: 875 us; the launch traced here: 864 us
  waiting for transfers between devices  600 us (69%)
  matrix products  101 us (12%)
  blocking collectives  59.9 us (7%)
  local copies, waits for them, and re-layouts  47.6 us (5%)
  other arithmetic  34.3 us (4%)
  between operations  20.3 us (2%)
    unnamed x10, waiting for transfers between devices  203 us
    reduce_scatter x1, waiting for transfers between devices, body(): lax.psum_scatter(outer_weight_grad.astype(jnp.bfloat16), 'fsdp', scatter_...  98.5 us
    reduce_scatter x1, waiting for transfers between devices, body(): lax.psum_scatter(inner_weight_grad.astype(jnp.bfloat16), 'fsdp', scatter_...  95.6 us
    all_gather x1, waiting for transfers between devices, body(): lax.all_gather(shards[2], 'fsdp', axis=0, tiled=True)  60 us
    all_gather x1, waiting for transfers between devices, body(): lax.all_gather(shards[1], 'fsdp', axis=0, tiled=True)  53.5 us
    all_gather x1, waiting for transfers between devices, body(): lax.all_gather(shards[0], 'fsdp', axis=1, tiled=True)  48 us
    psum x1, waiting for transfers between devices, body(): lax.psum(shard_grads[0].astype(jnp.bfloat16), 'dp').astype(jnp.float32)  41.6 us
    all_gather x1, blocking collectives, body(): lax.all_gather(shards[3], 'fsdp', axis=1, tiled=True)  32.4 us
  transfers between devices with their start and end apart: 8, of which 8 were waited for; matrix products, arithmetic and copies ran while one was open for 9% of the time, Pallas kernels for 0%

commit v1 on v0

--- a/solution.py
+++ b/solution.py
@@ -1,7 +1,160 @@
+import functools
+
 import jax
 import jax.numpy as jnp
 from jax import lax
 from jax.sharding import PartitionSpec as P
+
+from jax.experimental import pallas as pl
+from jax.experimental.pallas import tpu as pltpu
+
+MESH = pl.DeviceIdType.MESH
+NB = 6
+ALPHA = (1, 1, 1, 1, 0, 0)
+
+def place():
+    dp, f = lax.axis_index("dp"), lax.axis_index("fsdp")
+    return dp//2, dp%2, f//2, f%2
+
+class Gather:
+    def __init__(self, att, out, inn, sems, alpha):
+        self.att,self.out,self.inn=att,out,inn
+        self.zs,self.zr,self.ys,self.yr,self.xs,self.xr,self.cs,self.cr=sems
+        self.x,self.c,self.z,self.y=place()
+        self.alpha=alpha
+        self.started=[]
+    def dev(self,x=None,c=None,z=None,y=None):
+        x=self.x if x is None else x; c=self.c if c is None else c; z=self.z if z is None else z; y=self.y if y is None else y
+        return (x*2+c, z*2+y)
+    def ref(self,i,shard,cols,c=None):
+        c=self.c if c is None else c
+        cc=slice(None) if cols is None else pl.ds(pl.multiple_of(cols*384,128),384)
+        if i<2: return self.att.at[2*i+c,shard,:,cc]
+        if i<4: return self.out.at[shard,2*(i-2)+c,:,cc]
+        return self.inn.at[2*(i-4)+c,shard,:,cc]
+    def cp(self,r,ss,rs,dev):
+        return pltpu.make_async_remote_copy(src_ref=r,dst_ref=r,send_sem=ss,recv_sem=rs,device_id=dev,device_id_type=MESH)
+    def ccopy(self, i, recv=False):
+        c = 1 - self.c if recv else self.c
+        return self.cp(self.ref(i, slice(None), None, c), self.cs.at[i], self.cr.at[i], self.dev(c=1 - self.c))
+    def go(self, cp):
+        cp.start()
+    def zmove(self,i,s,right,shard,):
+        k=s if right else 3+s
+        d=jnp.minimum(self.z+1,3) if right else jnp.maximum(self.z-1,0)
+        return self.cp(self.ref(i,shard*2+self.y,self.x if self.alpha[i] else None),self.zs.at[i,k],self.zr.at[i,k],self.dev(z=d))
+    def yown(self,i): self.ymove(i,self.z).start()
+    def zown(self,i):
+        @pl.when(self.z<3)
+        def _(): self.zmove(i,0,True,self.z).start()
+        @pl.when(self.z>0)
+        def _(): self.zmove(i,0,False,self.z).start()
+    def ymove(self,i,sz,recv=False):
+        yy=1-self.y if recv else self.y
+        return self.cp(self.ref(i,sz*2+yy,self.x if self.alpha[i] else None),self.ys.at[i,sz],self.yr.at[i,sz],self.dev(y=1-self.y))
+    def xmove(self,i,sz,own,recv=False):
+        yy=self.y if own else 1-self.y
+        xx=1-self.x if recv else self.x
+        k=sz+(0 if own else 4)
+        return self.cp(self.ref(i,sz*2+yy,xx),self.xs.at[i,k],self.xr.at[i,k],self.dev(x=1-self.x))
+    def arrive(self,i,s):
+        z=self.z
+        @pl.when(z>=1+s)
+        def _():
+            sh=jnp.maximum(z-1-s,0)
+            self.zmove(i,s,True,sh).wait_recv()
+            if s<2:
+                @pl.when(z<3)
+                def _(): self.zmove(i,s+1,True,sh).start()
+            self.ymove(i,sh).start()
+            if self.alpha[i]: self.xmove(i,sh,True).start()
+        @pl.when(z+1+s<=3)
+        def _():
+            sh=jnp.minimum(z+1+s,3)
+            self.zmove(i,s,False,sh).wait_recv()
+            if s<2:
+                @pl.when(z>0)
+                def _(): self.zmove(i,s+1,False,sh).start()
+            self.ymove(i,sh).start()
+            if self.alpha[i]: self.xmove(i,sh,True).start()
+    def a0(self,i): self.arrive(i,0)
+    def a1(self,i): self.arrive(i,1)
+    def a2(self,i): self.arrive(i,2)
+    def third(self,i):
+        def one(sh):
+            self.ymove(i,sh,True).wait_recv()
+            if self.alpha[i]: self.xmove(i,sh,False).start()
+        one(self.z)
+        for s in range(3):
+            @pl.when(self.z>=1+s)
+            def _(): one(jnp.maximum(self.z-1-s,0))
+            @pl.when(self.z+1+s<=3)
+            def _(): one(jnp.minimum(self.z+1+s,3))
+    def fourth(self,i):
+        if self.alpha[i]:
+            for sz in range(4):
+                self.xmove(i,sz,False,True).wait_recv()
+                @pl.when(sz!=self.z)
+                def _(): self.xmove(i,sz,True,True).wait_recv()
+        self.go(self.ccopy(i))
+    def finish(self):
+        z=self.z
+        for i in range(NB):
+            for s in range(3):
+                @pl.when((z<3)&(z-s>=0))
+                def _(): self.zmove(i,s,True,jnp.maximum(z-s,0)).wait_send()
+                @pl.when((z>0)&(z+s<=3))
+                def _(): self.zmove(i,s,False,jnp.minimum(z+s,3)).wait_send()
+            for sz in range(4):
+                self.ymove(i,sz).wait_send()
+                if self.alpha[i]:
+                    self.xmove(i,sz,False).wait_send()
+                    @pl.when(sz!=z)
+                    def _(): self.xmove(i,sz,True).wait_send()
+            self.ccopy(i).wait_send()
+    def fifth(self,i): self.ccopy(i,True).wait_recv()
+
+def order_d(look,yl,d3,d4,d5,n=NB):
+    o=[]
+    for i in range(max(look,yl)):
+        if i<look: o.append(("zown",i))
+        if i<yl: o.append(("yown",i))
+    for t in range(n+d5):
+        for s in range(3):
+            if 0<=t-s<n: o.append((f"a{s}",t-s))
+        if t+look<n: o.append(("zown",t+look))
+        if t+yl<n: o.append(("yown",t+yl))
+        if 0<=t-d3<n: o.append(("third",t-d3))
+        if 0<=t-d4<n: o.append(("fourth",t-d4))
+        if 0<=t-d5<n: o.append(("fifth",t-d5))
+    return o
+
+def line_kernel(alpha,order,a,o,n,att,out,inn,*sems):
+    g=Gather(att,out,inn,sems,alpha)
+    me=g.z*2+g.y
+    for k in range(4):
+        att[k,me]=a[k]
+        out[me,k]=o[pl.ds(96*k,96),:]
+        inn[k,me]=n[:,768*k:768*k+768]
+    zr,zl=g.dev(z=jnp.minimum(g.z+1,3)),g.dev(z=jnp.maximum(g.z-1,0))
+    bar=pltpu.get_barrier_semaphore()
+    for d in (g.dev(y=1-g.y),g.dev(x=1-g.x),g.dev(c=1-g.c)): pl.semaphore_signal(bar,inc=1,device_id=d,device_id_type=MESH)
+    @pl.when(g.z<3)
+    def _(): pl.semaphore_signal(bar,inc=1,device_id=zr,device_id_type=MESH)
+    @pl.when(g.z>0)
+    def _(): pl.semaphore_signal(bar,inc=1,device_id=zl,device_id_type=MESH)
+    pl.semaphore_wait(bar,jnp.where((g.z==0)|(g.z==3),4,5))
+    steps = dict(zown=g.zown, yown=g.yown, a0=g.a0, a1=g.a1, a2=g.a2, third=g.third, fourth=g.fourth, fifth=g.fifth)
+    for s,i in order: steps[s](i)
+    g.finish()
+
+def gather_weights(a,o,n,alpha,order):
+    sems = [pltpu.SemaphoreType.DMA((NB,6)),pltpu.SemaphoreType.DMA((NB,6)),pltpu.SemaphoreType.DMA((NB,4)),pltpu.SemaphoreType.DMA((NB,4)),pltpu.SemaphoreType.DMA((NB,8)),pltpu.SemaphoreType.DMA((NB,8)),pltpu.SemaphoreType.DMA((NB,)),pltpu.SemaphoreType.DMA((NB,))]
+    vm=pl.BlockSpec(memory_space=pltpu.VMEM)
+    return tuple(pl.pallas_call(functools.partial(line_kernel,alpha,order),
+        out_shape=[jax.ShapeDtypeStruct((4,8,96,768),jnp.bfloat16),jax.ShapeDtypeStruct((8,4,96,768),jnp.bfloat16),jax.ShapeDtypeStruct((4,8,96,768),jnp.bfloat16)],
+        in_specs=[vm]*3,out_specs=[vm]*3,scratch_shapes=sems,
+        compiler_params=pltpu.CompilerParams(collective_id=0,has_side_effects=True,vmem_limit_bytes=60*2**20))(a,o,n))
 
 HEADS = 12
 STEP = 10
@@ -125,12 +278,20 @@
         outer_weight.astype(jnp.bfloat16),
         vectors.astype(jnp.bfloat16),
     )
-    attention_full, inner_full, outer_full, vector_full = (
-        lax.all_gather(shards[0], "fsdp", axis=1, tiled=True),
-        lax.all_gather(shards[1], "fsdp", axis=0, tiled=True),
-        lax.all_gather(shards[2], "fsdp", axis=0, tiled=True),
-        lax.all_gather(shards[3], "fsdp", axis=1, tiled=True),
-    )
+    vector_full = lax.all_gather(shards[3], "fsdp", axis=1, tiled=True)
+    if lax.axis_size("fsdp") == 8 and lax.axis_size("dp") == 4:
+        attention_full, outer_full, inner_full = gather_weights(
+            shards[0], shards[2], shards[1], ALPHA, order_d(2, 4, 3, 4, 5)
+        )
+        attention_full = attention_full.reshape(4, model_width, model_width)
+        outer_full = outer_full.reshape(-1, model_width)
+        inner_full = inner_full.reshape(4, model_width, -1).transpose(1, 0, 2).reshape(model_width, -1)
+    else:
+        attention_full, inner_full, outer_full = (
+            lax.all_gather(shards[0], "fsdp", axis=1, tiled=True),
+            lax.all_gather(shards[1], "fsdp", axis=0, tiled=True),
+            lax.all_gather(shards[2], "fsdp", axis=0, tiled=True),
+        )
     vector_rows = vector_full.astype(jnp.float32)
     bias_query = vector_rows[0]
     bias_value = vector_rows[1]
@@ -166,11 +327,7 @@
     sum_two = hidden_one + outer_pre
     output, norm_two_back = jax.vjp(layer_norm, sum_two, gain_two, shift_two)
     activations = output.astype(jnp.bfloat16).reshape(row_view)
-    attention_back, inner_back, outer_back = (
-        lax.all_gather(shards[0], "fsdp", axis=1, tiled=True),
-        lax.all_gather(shards[1], "fsdp", axis=0, tiled=True),
-        lax.all_gather(shards[2], "fsdp", axis=0, tiled=True),
-    )
+    attention_back, inner_back, outer_back = attention_full, inner_full, outer_full
     output_grad = cotangent.reshape(token_count, model_width).astype(jnp.float32)
     sum_two_grad, gain_two_grad, shift_two_grad = norm_two_back(output_grad)
     outer_grad = sum_two_grad.astype(jnp.bfloat16)

time: 875 us -> 772 us (0.88)
  waiting for transfers between devices: 600 us -> 444 us
  Pallas kernels: 0 us -> 66.5 us
    all_gather x3 -> x0, waiting for transfers between devices: 162 us -> none  [the longest x1 60 us: body(): lax.all_gather(shards[2], 'fsdp', axis=0, tiled=True)]
    pallas_call x0 -> x1, Pallas kernels: none -> 66.5 us  [gather_weights(): pl.pallas_call(functools.partial(line_kernel, alpha, order), out_shape=[j...]
    unnamed x103 -> x108, local copies, waits for them, and re-layouts: 19.6 us -> 13.7 us
    unnamed x10 -> x7, waiting for transfers between devices: 203 us -> 208 us
  transfers between devices with their start and end apart: 8 -> 5, of which waited for: 8 -> 5; matrix products, arithmetic and copies ran while one was open for 9% -> 3% of each run, Pallas kernels for 0% -> 0%
where the time goes in v1:
time: 772 us; the launch traced here: 765 us
  waiting for transfers between devices  444 us (58%)
  matrix products  94.2 us (12%)
  Pallas kernels  66.5 us (9%)
  blocking collectives  59.9 us (8%)
  local copies, waits for them, and re-layouts  43.8 us (6%)
  other arithmetic  37.4 us (5%)
  between operations  19.8 us (3%)
    unnamed x7, waiting for transfers between devices  208 us
    reduce_scatter x1, waiting for transfers between devices, body(): lax.psum_scatter(outer_weight_grad.astype(jnp.bfloat16), 'fsdp', scatter_...  98.7 us
    reduce_scatter x1, waiting for transfers between devices, body(): lax.psum_scatter(inner_weight_grad.astype(jnp.bfloat16), 'fsdp', scatter_...  95.8 us
    pallas_call x1, Pallas kernels, gather_weights(): pl.pallas_call(functools.partial(line_kernel, alpha, order), out_shape=[j...  66.5 us
    psum x1, waiting for transfers between devices, body(): lax.psum(shard_grads[0].astype(jnp.bfloat16), 'dp').astype(jnp.float32)  41.1 us
    all_gather x1, blocking collectives, body(): vector_full = lax.all_gather(shards[3], 'fsdp', axis=1, tiled=True)  32.2 us
    psum x1, blocking collectives, body(): total_squares = lax.psum(local_squares, 'fsdp')  21.8 us
    dot_general x1, matrix products, body(): jnp.dot(hidden_low, inner_full, preferred_element_type=jnp.float32)  20.4 us
  transfers between devices with their start and end apart: 5, of which 5 were waited for; matrix products, arithmetic and copies ran while one was open for 3% of the time, Pallas kernels for 0%

profile of v1, /device:TPU:0, one launch (start us, length us, event | category | flops | bytes accessed | tf_op | source)
XLA Modules:
  0.0 765.4 jit_solution(1284080654124750184)
XLA Ops:
  7.2 0.8 convert_bitcast_fusion
  8.0 32.2 %all-gather = bf16[8,96,12]{1,2,0:T(8,128)(2,1)S(1)} all-gather(bf16[1,96,12]{1,2,0:T(8,128)(2,1)S(1)} %convert_bitcast_fusion), channel_id=1, replica_groups=mesh['dp'=4,'fsdp'=8] {'fsdp'}, dimensions={0}, use_global_device_ids=true | all-gather | bytes 20736 | tf_op jit(solution)/shard_map/all_gather | solution.py:281
  40.4 2.2 convert_element_type.188.a
  42.6 0.9 convert_element_type.190.n
  43.5 0.9 convert_element_type.189.o
  44.4 66.5 %shard_map.279 = (bf16[4,8,96,768]{3,2,1,0:T(8,128)(2,1)}, bf16[8,4,96,768]{3,2,1,0:T(8,128)(2,1)}, bf16[4,8,96,768]{3,2,1,0:T(8,128)(2,1)}) custom-call(bf16[4,96,768]{2,1,0:T(8,128)(2,1)} %convert_element_type.188.a, bf16[384,768]{1,0:T(8,128)(2,1)} %convert_element_type.189.o, bf16[96,3072]{1,0:T(8,128)(2,1)} %convert_element_type.190.n), custom_call_target="tpu_custom_call" | custom-call | tf_op jit(solution)/shard_map/pallas_call | solution.py:154
  110.9 3.3 fusion.80
  114.6 0.9 copy-done.37
  115.5 2.1 convolution_bitcast_fusion
  117.7 1.4 fusion.81
  119.5 6.9 copy.89
  126.5 2.0 select_reduce_fusion
  128.5 2.2 fusion
  130.7 2.3 copy-done
  133.1 5.0 fusion.38
  138.1 1.0 fusion.82
  139.4 20.4 %multiply_convert_fusion.2 = (bf16[512,3072]{1,0:T(8,128)(2,1)S(1)}, f32[512,3072]{1,0:T(8,128)}, f32[512,3072]{1,0:T(8,128)}) fusion(f32[3072]{0:T(1024)S(1)} %add.224, bf16[768,3072]{0,1:T(8,128)(2,1)} %bitcast.100, f32[512,768]{1,0:T(8,128)S(1)} %get-tuple-element.170, f32[768]{0:T(1024)S(1)} %get-tuple-element.129, f32[768]{0:T(1024)S(1)} %get-tuple-element.130, ...), kind=kOutput, calls=%fused_computation.14 | convolution fusion | flops 2521694208 | bytes 22042624 | tf_op jit(solution)/shard_map/dot_general | solution.py:323
  159.8 2.8 fusion.83
  163.0 0.8 copy-done.2
  163.8 0.7 fusion.23
  164.5 1.6 fusion.78
  166.4 9.3 %fusion.75 = (bf16[3072]{0:T(1024)(128)(2,1)S(1)}, bf16[512,3072]{1,0:T(8,128)(2,1)}) fusion(f32[512,3072]{1,0:T(8,128)} %get-tuple-element.161, f32[512,3072]{1,0:T(8,128)} %get-tuple-element.171, f32[3072]{0:T(1024)S(1)} %add.224, bf16[512,768]{1,0:T(8,128)(2,1)S(1)} %get-tuple-element.151, bf16[3072,768]{1,0:T(8,128)(2,1)S(1)} %bitcast.126), kind=kOutput, calls=%fused_computation.146 | convolution fusion | flops 2441081856 | bytes 21252096 | tf_op jit(solution)/shard_map/td,fd->tf/dot_general | solution.py:338
  175.7 5.0 multiply_reduce_fusion.1
  180.7 0.6 fusion.77
  181.6 1.6 copy-done.24
  183.2 1.7 convolution_convert_fusion.3
  184.9 1.8 fusion.34
  186.8 2.3 copy.90
  189.1 7.9 %fusion.84 = (bf16[12,64]{1,0:T(8,128)(2,1)S(1)}, bf16[12,64,512]{2,1,0:T(8,128)(2,1)S(1)}) fusion(bf16[512,12,64]{0,2,1:T(8,128)(2,1)} %bitcast.106, f32[12,512,512]{1,2,0:T(8,128)} %copy-done, f32[12,512]{1,0:T(8,128)S(1)} %log_add_fusion, pred[512,512]{0,1:T(8,128)(4,1)S(1)} %broadcast_compare_fusion), kind=kOutput, calls=%fused_computation.154 | convolution fusion | flops 412876032 | bytes 14444032 | tf_op jit(solution)/shard_map/while/body/eval_jaxpr/hqk,qhe->khe/dot_general | solution.py:224
  197.0 9.6 %multiply_reduce_fusion = (f32[12,512]{1,0:T(8,128)S(1)}, f32[12,512,512]{1,2,0:T(8,128)}) fusion(f32[12,512,512]{1,2,0:T(8,128)} %copy-done, f32[12,512]{1,0:T(8,128)S(1)} %log_add_fusion, pred[512,512]{0,1:T(8,128)(4,1)S(1)} %broadcast_compare_fusion, bf16[512,12,64]{0,2,1:T(8,128)(2,1)S(1)} %bitcast.107, f32[512,12,64]{0,2,1:T(8,128)S(1)} %bitcast.99, ...), kind=kOutput, calls=%fused_computation.1 | convolution fusion | flops 416016384 | bytes 27839488 | tf_op jit(solution)/shard_map/while/body/eval_jaxpr/qhe,khe->hqk/dot_general | solution.py:221
  206.6 7.2 multiply_convert_fusion
  213.8 2.1 convolution_convert_fusion.4
  215.9 1.1 convert_reduce_fusion
  217.0 0.9 copy-done.16
  217.9 2.0 fusion.14
  219.9 2.6 pad_maximum_fusion
  222.5 8.5 %copy.97 = bf16[4,768,768]{2,0,1:T(4,128)(2,1)} copy(bf16[4,768,768]{1,2,0:T(8,128)(2,1)} %pad_maximum_fusion) | data formatting | bytes 9437184 | tf_op jit(solution)/shard_map/concatenate | solution.py:371
  231.1 1.3 copy-done.7
  232.4 6.5 convolution_convert_fusion.1
  239.0 1.1 copy-done.32
  240.1 6.7 convolution_convert_fusion
  247.5 0.8 copy.105
  249.6 151.0 %all-reduce.5.cloned.1.call-done = bf16[4,768,768]{2,0,1:T(4,128)(2,1)} async-done(((bf16[4,768,768]{2,0,1:T(4,128)(2,1)}), bf16[4,768,768]{2,0,1:T(4,128)(2,1)}) %all-reduce.5.cloned.1.call-update) | async-done | bytes 4718608
  400.6 1.3 constant_dynamic-slice_fusion
  401.9 0.9 copy.98
  402.8 95.8 %reduce-scatter.6.cloned.1.call-done = bf16[96,3072]{1,0:T(8,128)(2,1)} async-done(((bf16[768,3072]{1,0:T(8,128)(2,1)}), bf16[96,3072]{1,0:T(8,128)(2,1)}) %reduce-scatter.6.cloned.1.call-update) | async-done | bytes 589840 | tf_op jit(solution)/shard_map/reduce_scatter | solution.py:395
  498.5 98.7 %reduce-scatter.8.cloned.1.call-done = bf16[384,768]{1,0:T(8,128)(2,1)} async-done(((bf16[3072,768]{1,0:T(8,128)(2,1)}), bf16[384,768]{1,0:T(8,128)(2,1)}) %reduce-scatter.8.cloned.1.call-update) | async-done | bytes 589840 | tf_op jit(solution)/shard_map/reduce_scatter | solution.py:398
  597.3 3.3 slice.76
  600.6 1.2 copy.95
  601.7 1.2 copy.94
  602.9 2.0 fusion.85
  604.9 56.9 %reduce-scatter.10.cloned.1.call-done = bf16[96,12]{1,0:T(8,128)(2,1)} async-done(((bf16[768,12]{1,0:T(8,128)(2,1)}), bf16[96,12]{1,0:T(8,128)(2,1)}) %reduce-scatter.10.cloned.1.call-update) | async-done | bytes 2320
  661.8 0.8 copy.106
  662.6 5.9 psum.38
  669.1 41.1 %all-reduce.7.cloned.1.call-done = (bf16[4,96,768]{2,1,0:T(8,128)(2,1)}, bf16[96,3072]{1,0:T(8,128)(2,1)}, bf16[384,768]{1,0:T(8,128)(2,1)}) async-done(((bf16[4,96,768]{2,1,0:T(8,128)(2,1)}, bf16[96,3072]{1,0:T(8,128)(2,1)}, bf16[384,768]{1,0:T(8,128)(2,1)}), (bf16[4,96,768]{2,1,0:T(8,128)(2,1)}, bf16[96,3072]{1,0:T(8,128)(2,1)}, bf16[384,768]{1,0:T(8,128)(2,1)})) %all-reduce.7.cloned.1.call-update) | async-done | bytes 1769488 | tf_op jit(solution)/shard_map/psum | solution.py:406
  710.2 2.0 fusion.45
  712.2 2.0 fusion.44
  714.2 2.0 fusion.43
  718.8 5.3 fusion.28
  724.1 21.8 %psum.39 = f32[]{:T(128)} all-reduce(f32[]{:T(128)S(6)} %add.241), channel_id=1, replica_groups=mesh['dp'=4,'fsdp'=8] {'fsdp'}, use_global_device_ids=true, to_apply=%region_32.33 | all-reduce | flops 1 | bytes 8 | tf_op jit(solution)/shard_map/psum | solution.py:417
  747.4 4.2 multiply_subtract_fusion
  751.6 2.4 multiply_subtract_fusion.1
  754.4 0.6 copy-done.28
  755.0 2.4 multiply_subtract_fusion.2
  (147 shorter events, 5.3 us)
Async XLA Ops:
  7.2 35.5 %copy-start.10 = (f32[96,3072]{1,0:T(8,128)S(1)}, f32[96,3072]{1,0:T(8,128)}, u32[]{:S(2)}) copy-start(f32[96,3072]{1,0:T(8,128)} %param.22) | copy-start | bytes 3538948
  7.2 393.4 %all-reduce.5.cloned.1.call-start = ((), (), s32[]{:S(2)}) async-start(), calls=%async_computation.6 | async-start | bytes 9437184
  40.4 3.1 copy-start.8
  110.9 3.5 copy-start.1
  114.4 1.1 copy-start.37
  117.7 1.6 copy-start.34
  128.5 4.6 copy-start
  133.1 5.0 copy-start.23
  133.1 5.0 copy-start.38
  138.1 1.0 copy-start.40
  138.1 21.7 %slice-start.5 = ((s8[4718592]{0:T(1024)(128)(4,1)}), s8[4194304]{0:T(1024)(128)(4,1)S(1)}, s32[]{:S(2)}) async-start(s8[4718592]{0:T(1024)(128)(4,1)} %bitcast.123), calls=%async_computation.13 | async-start | bytes 8388608
  139.1 41.7 %copy-start.6 = (f32[512,768]{1,0:T(8,128)}, f32[512,768]{1,0:T(8,128)S(1)}, u32[]{:S(2)}) copy-start(f32[512,768]{1,0:T(8,128)S(1)} %get-tuple-element.170) | copy-start | bytes 4718596
  139.4 20.4 %slice-start.6 = ((s8[4718592]{0:T(1024)(128)(4,1)}), s8[524288]{0:T(1024)(128)(4,1)S(1)}, s32[]{:S(2)}) async-start(s8[4718592]{0:T(1024)(128)(4,1)} %bitcast.123), calls=%async_computation.14 | async-start | bytes 1048576
  159.8 2.8 copy-start.44
  162.6 1.1 copy-start.2
  164.5 11.1 %slice-start.3 = ((s8[4718592]{0:T(1024)(128)(4,1)}), s8[4194304]{0:T(1024)(128)(4,1)S(1)}, s32[]{:S(2)}) async-start(s8[4718592]{0:T(1024)(128)(4,1)} %bitcast.101), calls=%async_computation.11 | async-start | bytes 8388608
  166.4 9.3 %copy-start.31 = (bf16[512,768]{1,0:T(8,128)(2,1)}, bf16[512,768]{1,0:T(8,128)(2,1)S(1)}, u32[]{:S(2)}) copy-start(bf16[512,768]{1,0:T(8,128)(2,1)S(1)} %get-tuple-element.151) | copy-start | bytes 2359300
  166.4 9.3 %slice-start.4 = ((s8[4718592]{0:T(1024)(128)(4,1)}), s8[524288]{0:T(1024)(128)(4,1)S(1)}, s32[]{:S(2)}) async-start(s8[4718592]{0:T(1024)(128)(4,1)} %bitcast.101), calls=%async_computation.12 | async-start | bytes 1048576
  181.4 3.5 copy-start.4
  181.4 1.8 copy-start.24
  183.2 1.7 copy-start.41
  189.1 7.9 %copy-start.3 = (f32[1,512,768]{1,2,0:T(8,128)S(1)}, f32[1,512,768]{1,2,0:T(8,128)}, u32[]{:S(2)}) copy-start(f32[1,512,768]{1,2,0:T(8,128)} %get-tuple-element.164) | copy-start | bytes 4718596
  189.1 7.9 %copy-start.13 = (bf16[512,768]{0,1:T(8,128)(2,1)S(1)}, bf16[512,768]{0,1:T(8,128)(2,1)}, u32[]{:S(2)}) copy-start(bf16[512,768]{0,1:T(8,128)(2,1)} %copy.90) | copy-start | bytes 2359300
  189.1 17.5 %slice-start = ((s8[12582912]{0:T(1024)(128)(4,1)}), s8[4194304]{0:T(1024)(128)(4,1)S(1)}, s32[]{:S(2)}) async-start(s8[12582912]{0:T(1024)(128)(4,1)} %bitcast.92), calls=%async_computation.8 | async-start | bytes 8388608
  189.1 17.5 %slice-start.1 = ((s8[12582912]{0:T(1024)(128)(4,1)}), s8[4194304]{0:T(1024)(128)(4,1)S(1)}, s32[]{:S(2)}) async-start(s8[12582912]{0:T(1024)(128)(4,1)} %bitcast.92), calls=%async_computation.9 | async-start | bytes 8388608
  196.9 20.1 %copy-start.29 = (bf16[12,64,512]{2,1,0:T(8,128)(2,1)}, bf16[12,64,512]{2,1,0:T(8,128)(2,1)S(1)}, u32[]{:S(2)}) copy-start(bf16[12,64,512]{2,1,0:T(8,128)(2,1)S(1)} %get-tuple-element.180) | copy-start | bytes 2359300
  197.0 9.6 %slice-start.2 = ((s8[12582912]{0:T(1024)(128)(4,1)}), s8[4194304]{0:T(1024)(128)(4,1)S(1)}, s32[]{:S(2)}) async-start(s8[12582912]{0:T(1024)(128)(4,1)} %bitcast.92), calls=%async_computation.10 | async-start | bytes 8388608
  215.8 1.2 copy-start.14
  215.8 2.1 copy-start.39
  215.9 2.1 copy-start.43
  217.0 0.9 copy-start.16
  217.9 2.0 copy-start.21
  231.0 1.4 copy-start.7
  231.1 267.5 %reduce-scatter.6.cloned.1.call-start = ((), (), s32[]{:S(2)}) async-start(), calls=%async_computation.3 | async-start | bytes 5308416 | tf_op jit(solution)/shard_map/reduce_scatter | solution.py:395
  239.0 1.1 copy-start.32
  239.0 358.2 %reduce-scatter.8.cloned.1.call-start = ((), (), s32[]{:S(2)}) async-start(), calls=%async_computation.4 | async-start | bytes 5308416 | tf_op jit(solution)/shard_map/reduce_scatter | solution.py:398
  246.8 1.6 copy-start.42
  246.8 415.0 %reduce-scatter.10.cloned.1.call-start = ((), (), s32[]{:S(2)}) async-start(), calls=%async_computation.5 | async-start | bytes 221184
  248.3 461.9 %all-reduce.7.cloned.1.call-start = ((), (), s32[]{:S(2)}) async-start(), calls=%async_computation.7 | async-start | bytes 3538944 | tf_op jit(solution)/shard_map/psum | solution.py:406
  597.3 3.3 copy-start.30
  600.6 1.2 copy-start.15
  600.6 2.3 copy-start.17
  600.6 2.3 copy-start.22
  604.9 113.9 %copy-start.5 = (f32[512,768]{1,0:T(8,128)S(1)}, f32[512,768]{1,0:T(8,128)}, u32[]{:S(2)}) copy-start(f32[512,768]{1,0:T(8,128)} %copy-done.4) | copy-start | bytes 4718596
  718.8 27.9 %copy-start.33 = (f32[12,96]{1,0:T(8,128)S(1)}, f32[12,96]{1,0:T(8,128)}, u32[]{:S(2)}) copy-start(f32[12,96]{1,0:T(8,128)} %param.28) | copy-start | bytes 13828
  718.8 27.9 %copy-start.35 = (f32[12,96]{1,0:T(8,128)S(1)}, f32[12,96]{1,0:T(8,128)}, u32[]{:S(2)}) copy-start(f32[12,96]{1,0:T(8,128)} %param.29) | copy-start | bytes 13828
  718.8 27.9 %copy-start.36 = (f32[12,96]{1,0:T(8,128)S(1)}, f32[12,96]{1,0:T(8,128)}, u32[]{:S(2)}) copy-start(f32[12,96]{1,0:T(8,128)} %param.30) | copy-start | bytes 13828
  718.8 28.6 %copy-start.9 = (f32[384,768]{1,0:T(8,128)S(1)}, f32[384,768]{1,0:T(8,128)}, u32[]{:S(2)}) copy-start(f32[384,768]{1,0:T(8,128)} %param.25) | copy-start | bytes 3538948
  718.8 28.5 %copy-start.20 = (bf16[384,768]{1,0:T(8,128)(2,1)S(1)}, bf16[384,768]{1,0:T(8,128)(2,1)}, u32[]{:S(2)}) copy-start(bf16[384,768]{1,0:T(8,128)(2,1)} %get-tuple-element.136) | copy-start | bytes 1769476
  747.3 4.2 copy-start.11
  747.4 4.2 copy-start.19
  747.4 4.2 copy-start.25
  747.4 4.2 copy-start.26
  751.6 2.5 copy-start.12
  751.6 2.5 copy-start.18
  751.6 2.8 copy-start.27
  751.6 3.4 copy-start.28
Sparse Core Ops, SparseCore 0:
  231.2 169.3 all-reduce.4
  404.3 94.2 reduce-scatter.5
  502.2 94.9 reduce-scatter.7
  600.9 60.8 reduce-scatter.9
  664.8 45.4 all-reduce.6

commit v2 on v0

--- a/solution.py
+++ b/solution.py
@@ -1,6 +1,10 @@
+import functools
+
 import jax
 import jax.numpy as jnp
 from jax import lax
+from jax.experimental import pallas as pl
+from jax.experimental.pallas import tpu as pltpu
 from jax.sharding import PartitionSpec as P
 
 HEADS = 12
@@ -99,7 +103,844 @@
     return (weight_new, first_new, second_new)
 
 
-def body(
+F32, BF16 = jnp.float32, jnp.bfloat16
+MESH = pl.DeviceIdType.MESH
+BLOCKS = 6
+CHUNKS = 6
+INV_SQRT2 = 0.7071067811865476
+INV_SQRT2PI = 0.3989422804014327
+
+
+def dot_nn(a, b):
+    return lax.dot_general(a, b, (((1,), (0,)), ((), ())), preferred_element_type=F32)
+
+
+def dot_nt(a, b):
+    return lax.dot_general(a, b, (((1,), (1,)), ((), ())), preferred_element_type=F32)
+
+
+def dot_tn(a, b):
+    return lax.dot_general(a, b, (((0,), (0,)), ((), ())), preferred_element_type=F32)
+
+
+def wide(value):
+    return value.astype(F32)
+
+
+class Place:
+    def __init__(self):
+        dp, fsdp = lax.axis_index("dp"), lax.axis_index("fsdp")
+        self.x, self.c, self.z, self.y = dp // 2, dp % 2, fsdp // 2, fsdp % 2
+
+    def dev(self, x=None, c=None, z=None, y=None):
+        x = self.x if x is None else x
+        c = self.c if c is None else c
+        z = self.z if z is None else z
+        y = self.y if y is None else y
+        return (x * 2 + c, z * 2 + y)
+
+    def far(self, dz):
+        return lax.rem(self.z + dz, 4)
+
+
+def half(x):
+    return pl.ds(pl.multiple_of(x * 384, 128), 384)
+
+
+def remote(src, dst, send, recv, dev):
+    return pltpu.make_async_remote_copy(
+        src_ref=src, dst_ref=dst, send_sem=send, recv_sem=recv, device_id=dev, device_id_type=MESH
+    )
+
+
+class Gather:
+    def __init__(self, at, att, inn, out, sems, alpha):
+        self.at, self.att, self.inn, self.out, self.alpha = at, att, inn, out, alpha
+        self.zs, self.zr, self.ys, self.yr, self.xs, self.xr, self.cs, self.cr = sems
+
+    def ref(self, i, z, y, x, c=None):
+        c = self.at.c if c is None else c
+        cols = half(x) if self.alpha[i] else slice(None)
+        if i < 2:
+            return self.att.at[2 * i + c, z, y, :, cols]
+        if i < 4:
+            return self.inn.at[2 * (i - 2) + c, z, y, :, cols]
+        return self.out.at[z, y, 2 * (i - 4) + c, :, cols]
+
+    def whole(self, i, c):
+        if i < 2:
+            return self.att.at[2 * i + c]
+        if i < 4:
+            return self.inn.at[2 * (i - 2) + c]
+        return self.out.at[:, :, 2 * (i - 4) + c]
+
+    def zmove(self, i, s, right, sz):
+        k = s if right else 3 + s
+        z = self.at.z
+        dest = jnp.minimum(z + 1, 3) if right else jnp.maximum(z - 1, 0)
+        r = self.ref(i, sz, self.at.y, self.at.x)
+        return remote(r, r, self.zs.at[i, k], self.zr.at[i, k], self.at.dev(z=dest))
+
+    def ymove(self, i, sz, recv=False):
+        y = 1 - self.at.y if recv else self.at.y
+        r = self.ref(i, sz, y, self.at.x)
+        return remote(r, r, self.ys.at[i, sz], self.yr.at[i, sz], self.at.dev(y=1 - self.at.y))
+
+    def xmove(self, i, sz, own, recv=False):
+        y = self.at.y if own else 1 - self.at.y
+        x = 1 - self.at.x if recv else self.at.x
+        k = sz + (0 if own else 4)
+        r = self.ref(i, sz, y, x)
+        return remote(r, r, self.xs.at[i, k], self.xr.at[i, k], self.at.dev(x=1 - self.at.x))
+
+    def cmove(self, i, recv=False):
+        r = self.whole(i, 1 - self.at.c if recv else self.at.c)
+        return remote(r, r, self.cs.at[i], self.cr.at[i], self.at.dev(c=1 - self.at.c))
+
+    def zown(self, i):
+        z = self.at.z
+
+        @pl.when(z < 3)
+        def _():
+            self.zmove(i, 0, True, z).start()
+
+        @pl.when(z > 0)
+        def _():
+            self.zmove(i, 0, False, z).start()
+
+    def yown(self, i):
+        self.ymove(i, self.at.z).start()
+
+    def arrive(self, i, s):
+        z = self.at.z
+
+        def forward(sz, right, more):
+            self.zmove(i, s, right, sz).wait_recv()
+            if s < 2:
+
+                @pl.when(more)
+                def _():
+                    self.zmove(i, s + 1, right, sz).start()
+
+            self.ymove(i, sz).start()
+            if self.alpha[i]:
+                self.xmove(i, sz, True).start()
+
+        @pl.when(z >= 1 + s)
+        def _():
+            forward(jnp.maximum(z - 1 - s, 0), True, z < 3)
+
+        @pl.when(z + 1 + s <= 3)
+        def _():
+            forward(jnp.minimum(z + 1 + s, 3), False, z > 0)
+
+    def across(self, i, s):
+        z = self.at.z
+
+        def one(sz):
+            self.ymove(i, sz, True).wait_recv()
+            if self.alpha[i]:
+                self.xmove(i, sz, False).start()
+
+        if s == 0:
+            one(z)
+            return
+
+        @pl.when(z >= s)
+        def _():
+            one(jnp.maximum(z - s, 0))
+
+        @pl.when(z + s <= 3)
+        def _():
+            one(jnp.minimum(z + s, 3))
+
+    def join(self, i):
+        if self.alpha[i]:
+            for sz in range(4):
+                self.xmove(i, sz, False, True).wait_recv()
+
+                @pl.when(sz != self.at.z)
+                def _():
+                    self.xmove(i, sz, True, True).wait_recv()
+
+        self.cmove(i).start()
+
+    def have(self, i):
+        self.cmove(i, True).wait_recv()
+
+    def finish(self):
+        z = self.at.z
+        for i in range(BLOCKS):
+            for s in range(3):
+
+                @pl.when((z < 3) & (z - s >= 0))
+                def _():
+                    self.zmove(i, s, True, jnp.maximum(z - s, 0)).wait_send()
+
+                @pl.when((z > 0) & (z + s <= 3))
+                def _():
+                    self.zmove(i, s, False, jnp.minimum(z + s, 3)).wait_send()
+
+            for sz in range(4):
+                self.ymove(i, sz).wait_send()
+                if self.alpha[i]:
+                    self.xmove(i, sz, False).wait_send()
+
+                    @pl.when(sz != z)
+                    def _():
+                        self.xmove(i, sz, True).wait_send()
+
+            self.cmove(i).wait_send()
+
+
+class Scatter:
+    def __init__(self, at, grad, total, bufs, sems, alpha):
+        self.at, self.grad, self.total, self.alpha = at, grad, total, alpha
+        self.ra1, self.ra2, self.ra3, self.rb1, self.rb2, self.rb3 = bufs
+        self.ss, self.rs = sems
+        self.slot = [sum(1 for q in alpha[:j] if q == alpha[j]) for j in range(CHUNKS)]
+
+    def cp(self, j, k, src, dst, dev):
+        return remote(src, dst, self.ss.at[j, k], self.rs.at[j, k], dev)
+
+    def block(self, j, c):
+        return 4 * (j // 2) + 2 * c + j % 2
+
+    def firsts(self, j, dz, own):
+        n, at = self.slot[j], self.at
+        z = at.far(dz)
+        if self.alpha[j]:
+            y = at.y if own else 1 - at.y
+            return self.cp(
+                j, dz + 4 * own, self.grad(j, z, y).at[:, half(1 - at.x)], self.ra1.at[n, z, y], at.dev(x=1 - at.x)
+            )
+        return self.cp(j, dz, self.grad(j, z, 1 - at.y), self.rb1.at[n, z], at.dev(y=1 - at.y))
+
+    def second(self, j, dz):
+        n, at = self.slot[j], self.at
+        z = at.far(dz)
+        return self.cp(
+            j, 8 + dz, self.grad(j, z, 1 - at.y).at[:, half(at.x)], self.ra2.at[n, z], at.dev(y=1 - at.y)
+        )
+
+    def third(self, j, dz):
+        n, at = self.slot[j], self.at
+        z = at.far(dz)
+        src = self.grad(j, z, at.y)
+        if self.alpha[j]:
+            return self.cp(j, 11 + dz, src.at[:, half(at.x)], self.ra3.at[n, dz - 1], at.dev(z=z))
+        return self.cp(j, 11 + dz, src, self.rb2.at[n, dz - 1], at.dev(z=z))
+
+    def fourth(self, j, recv=False):
+        n, at = self.slot[j], self.at
+        if self.alpha[j]:
+            r = self.total.at[self.block(j, at.c), :, half(1 - at.x if recv else at.x)]
+            return self.cp(j, 15, r, r, at.dev(x=1 - at.x))
+        return self.cp(j, 15, self.grad(j, at.z, at.y), self.rb3.at[n], at.dev(x=1 - at.x))
+
+    def fifth(self, j, recv=False):
+        r = self.total.at[self.block(j, 1 - self.at.c if recv else self.at.c)]
+        return self.cp(j, 16, r, r, self.at.dev(c=1 - self.at.c))
+
+    def s1(self, j):
+        for dz in (2, 1, 3, 0):
+            self.firsts(j, dz, 0).start()
+
+    def r1(self, j):
+        if self.alpha[j]:
+            for dz in (2, 1, 3, 0):
+                self.firsts(j, dz, 1).start()
+
+    def p(self, j, dz):
+        if not self.alpha[j]:
+            return
+        n, at = self.slot[j], self.at
+        z, y, h = at.far(dz), 1 - at.y, half(at.x)
+        self.firsts(j, dz, 0).wait_recv()
+        r = self.grad(j, z, y)
+        r[:, h] = (wide(r[:, h]) + wide(self.ra1[n, z, y])).astype(BF16)
+        self.second(j, dz).start()
+
+    def q(self, j, dz):
+        n, at = self.slot[j], self.at
+        z, y, h = at.far(dz), at.y, half(at.x)
+        r = self.grad(j, z, y)
+        if self.alpha[j]:
+            self.firsts(j, dz, 1).wait_recv()
+            self.second(j, dz).wait_recv()
+            r[:, h] = (wide(r[:, h]) + wide(self.ra1[n, z, y]) + wide(self.ra2[n, z])).astype(BF16)
+        else:
+            self.firsts(j, dz, 0).wait_recv()
+            r[...] = (wide(r[...]) + wide(self.rb1[n, z])).astype(BF16)
+        if dz:
+            self.third(j, dz).start()
+
+    def s4(self, j):
+        n, at = self.slot[j], self.at
+        for dz in (1, 2, 3):
+            self.third(j, dz).wait_recv()
+        r = self.grad(j, at.z, at.y)
+        if self.alpha[j]:
+            h = half(at.x)
+            total = wide(r[:, h])
+            for dz in range(3):
+                total = total + wide(self.ra3[n, dz])
+            self.total[self.block(j, at.c), :, h] = total.astype(BF16)
+        else:
+            total = wide(r[...])
+            for dz in range(3):
+                total = total + wide(self.rb2[n, dz])
+            r[...] = total.astype(BF16)
+        self.fourth(j).start()
+
+    def s5(self, j):
+        n, at = self.slot[j], self.at
+        self.fourth(j, True).wait_recv()
+        if not self.alpha[j]:
+            r = self.grad(j, at.z, at.y)
+            self.total[self.block(j, at.c)] = (wide(r[...]) + wide(self.rb3[n])).astype(BF16)
+        self.fifth(j).start()
+
+    def s6(self, j):
+        self.fifth(j, True).wait_recv()
+
+    def finish(self):
+        for j in range(CHUNKS):
+            for dz in range(4):
+                self.firsts(j, dz, 0).wait_send()
+                if self.alpha[j]:
+                    self.firsts(j, dz, 1).wait_send()
+                    self.second(j, dz).wait_send()
+                if dz:
+                    self.third(j, dz).wait_send()
+            self.fourth(j).wait_send()
+            self.fifth(j).wait_send()
+
+
+def layer_kernel(
+    order, alpha_gather, alpha_scatter,
+    tok_h, cot_h, seg_row, watt_h, winn_h, wout_h, vec_in,
+    act_h, grad_h, total, vec_grad, norm,
+    att, inn, out, norm_one, resid, work, pair_in, stack, hidden, outer_grad, shown, turn, turn_two,
+    active, slope, probs, mask, vec, dev_one, dev_two,
+    sib_in, sib_hidden, sib_active, sib_outer, sib_slope, sib_stack,
+    grad_out, ra1, ra2, ra3, rb1, rb2, rb3,
+    vec_parts, vec_sib, vec_x, vec_y, vec_z, norm_parts,
+    zs, zr, ys, yr, xs, xr, cs, cr, ss, rs, bs, br, vs, vr, ws, wr, ns, nr, ls,
+):
+    at = Place()
+    me = at.z * 2 + at.y
+    ag = Gather(at, att, inn, out, (zs, zr, ys, yr, xs, xr, cs, cr), alpha_gather)
+
+    def grad_ref(j, z, y):
+        return grad_out.at[j, z, y] if j < 2 else out.at[z, y, j - 2]
+
+    rd = Scatter(at, grad_ref, total, (ra1, ra2, ra3, rb1, rb2, rb3), (ss, rs), alpha_scatter)
+
+    def square(ref, n=768):
+        return ref[...].reshape(n, n)
+
+    other = at.dev(c=1 - at.c)
+
+    def to_sibling(k, src, dst):
+        return remote(src, dst, bs.at[k], br.at[k], other)
+
+    sib_tokens = to_sibling(0, pair_in.at[0], sib_in.at[0])
+    sib_context = to_sibling(1, pair_in.at[1], sib_in.at[1])
+    sib_hid = to_sibling(2, hidden, sib_hidden)
+    sib_act = to_sibling(3, active.at[:, :, pl.ds(2 * (1 - at.c), 2)], sib_active)
+    sib_og = to_sibling(4, outer_grad, sib_outer)
+    sib_sl = to_sibling(5, slope.at[:, pl.ds(pl.multiple_of((1 - at.c) * 1536, 128), 1536)], sib_slope)
+    sib_first = to_sibling(6, stack.at[1 - at.c], sib_stack.at[0])
+    sib_last = to_sibling(7, stack.at[3 - at.c], sib_stack.at[1])
+
+    peers = [(dz, dy) for dz in range(4) for dy in range(2) if (dz, dy) != (0, 0)]
+
+    def peer(dz, dy):
+        return at.dev(z=at.far(dz), y=lax.rem(at.y + dy, 2))
+
+    def vec_move(k, recv=False):
+        dz, dy = peers[k]
+        s = lax.rem(at.z + 4 - dz, 4) * 2 + lax.rem(at.y + dy, 2) if recv else me
+        return remote(vec_parts.at[s], vec_parts.at[s], vs.at[k], vr.at[k], peer(dz, dy))
+
+    def norm_move(k, recv=False):
+        dz, dy = peers[k]
+        s = lax.rem(at.z + 4 - dz, 4) * 2 + lax.rem(at.y + dy, 2) if recv else me
+        return remote(norm_parts.at[s], norm_parts.at[s], ns.at[k], nr.at[k], peer(dz, dy))
+
+    loads = [pltpu.make_async_copy(watt_h.at[k], norm_one.at[pl.ds(96 * k, 96)], ls.at[k]) for k in range(4)]
+    loads += [
+        pltpu.make_async_copy(winn_h.at[:, pl.ds(768 * k, 768)], work.at[pl.ds(96 * k, 96)], ls.at[4 + k])
+        for k in range(4)
+    ]
+    loads += [pltpu.make_async_copy(wout_h, resid.at[pl.ds(0, 384)], ls.at[8])]
+    load_tokens = pltpu.make_async_copy(tok_h, pair_in.at[0], ls.at[9])
+    load_cotangent = pltpu.make_async_copy(cot_h, stack.at[3], ls.at[10])
+    store_shown = pltpu.make_async_copy(shown, act_h, ls.at[11])
+    store_grad = pltpu.make_async_copy(work, grad_h, ls.at[12])
+
+    def init():
+        for cp in loads:
+            cp.start()
+        load_tokens.start()
+        load_cotangent.start()
+        barrier = pltpu.get_barrier_semaphore()
+        greet = [peer(dz, dy) for dz, dy in peers] + [at.dev(x=1 - at.x), other]
+        for d in greet:
+            pl.semaphore_signal(barrier, inc=1, device_id=d, device_id_type=MESH)
+        for cp in loads:
+            cp.wait()
+        for i in range(2):
+            k = 2 * i + at.c
+            rows = pl.ds(pl.multiple_of(96 * k, 96), 96)
+            att[k, at.z, at.y] = norm_one[rows, :].astype(BF16)
+            inn[k, at.z, at.y] = work[rows, :].astype(BF16)
+            out[at.z, at.y, k] = resid[rows, :].astype(BF16)
+        vec_parts[me] = jnp.zeros((16, 128), F32)
+        vec_parts[me, :12, :96] = vec_in[...]
+        vec_grad[...] = jnp.zeros_like(vec_grad)
+        pl.semaphore_wait(barrier, len(greet))
+
+    def early():
+        for k in range(7):
+            vec_move(k).start()
+        load_tokens.wait()
+        sib_tokens.start()
+        ids = jnp.broadcast_to(seg_row[...].astype(F32), (512, 512))
+        mask[...] = jnp.where(ids.T == ids, 1.0, 0.0)
+
+    def vectors_here():
+        for k in range(7):
+            vec_move(k, True).wait_recv()
+        full = jnp.zeros((16, 768), F32)
+        row = lax.broadcasted_iota(jnp.int32, (128, 768), 0)
+        col = lax.broadcasted_iota(jnp.int32, (128, 768), 1)
+        for s in range(8):
+            pick = jnp.where((col == row + 96 * s) & (row < 96), 1.0, 0.0).astype(BF16)
+            full = full + dot_nn(vec_parts[s].astype(BF16), pick)
+        vec[...] = full
+
+    def vrow(r):
+        return vec[pl.ds(r, 1), :]
+
+    def queries_keys():
+        tokens = pair_in[0]
+        stack[0] = ((dot_nn(tokens, square(att.at[0])) + vrow(0)) * 0.125).astype(BF16)
+        stack[2] = dot_nn(tokens, square(att.at[1])).astype(BF16)
+
+    def values():
+        stack[1] = (dot_nn(pair_in[0], square(att.at[2])) + vrow(1)).astype(BF16)
+
+    low = lax.broadcasted_iota(jnp.int32, (512, 128), 1) < 64
+
+    def attend(p):
+        ls_ = pl.ds(128 * p, 128)
+        queries, keys = stack[0, :, ls_], stack[2, :, ls_]
+        values_t = stack[1, :, ls_].T
+        for h in range(2):
+            mine = jnp.where(low if h == 0 else ~low, keys, jnp.zeros_like(keys))
+            scores = jnp.where(mask[...] > 0.5, dot_nt(mine, queries), -1000000000.0)
+            peak = jnp.max(scores, axis=0, keepdims=True)
+            exponent = jnp.exp(scores - peak)
+            scale = 1.0 / jnp.sum(exponent, axis=0, keepdims=True)
+            weights = (exponent * scale).astype(BF16)
+            probs[2 * p + h] = weights
+            turn[pl.ds(128 * p + 64 * h, 64), :] = dot_nn(values_t[64 * h : 64 * h + 64], weights).astype(BF16)
+
+    def norm_stats(value):
+        centre = jnp.mean(value, axis=1, keepdims=True)
+        centered = value - centre
+        spread = jnp.mean(centered * centered, axis=1, keepdims=True)
+        scale = lax.rsqrt(spread + EPS_NORM)
+        return centered * scale, scale
+
+    def project_out():
+        pair_in[1] = turn[...].T
+        sib_context.start()
+        resid[...] = wide(pair_in[0]) + dot_nn(pair_in[1], square(att.at[3])) + vrow(2)
+        for r in range(4):
+            rows = pl.ds(128 * r, 128)
+            normed, scale = norm_stats(resid[rows, :])
+            norm_one[rows, :] = normed
+            dev_one[rows, :] = scale
+            hidden[rows, :] = (normed * vrow(3) + vrow(4)).astype(BF16)
+        sib_hid.start()
+
+    def feed_in(q):
+        work[...] = dot_nn(hidden[...], square(inn.at[q])) + vrow(5 + q)
+        for r in range(4):
+            rows = pl.ds(128 * r, 128)
+            value = work[rows, :]
+            share = 0.5 * (1.0 + lax.erf(value * INV_SQRT2))
+            shown[rows, :] = (value * share).astype(BF16)
+            density = jnp.exp(-0.5 * value * value) * INV_SQRT2PI
+            slope[rows, 768 * q : 768 * q + 768] = (share + value * density).astype(BF16)
+        active[q] = shown[...].T.reshape(2, 4, 96, 512)
+
+    def feed_out():
+        sib_act.start()
+        for n in range(3):
+            cols = slice(256 * n, 256 * n + 256)
+            value = norm_one[:, cols] * vec[3:4, cols] + vec[4:5, cols] + vec[9:10, cols]
+            for q in range(4):
+                value = value + dot_tn(
+                    active[q].reshape(768, 512), out[q, :, :, :, cols].reshape(768, 256)
+                )
+            resid[:, cols] = value
+
+    def end_norm():
+        load_cotangent.wait()
+        sums = [jnp.zeros((1, 768), F32) for _ in range(3)]
+        for r in range(4):
+            rows = pl.ds(128 * r, 128)
+            normed, scale = norm_stats(resid[rows, :])
+            shown[rows, :] = (normed * vrow(10) + vrow(11)).astype(BF16)
+            given = wide(stack[3, rows, :])
+            scaled = given * vrow(10)
+            back = scale * (
+                scaled
+                - jnp.mean(scaled, axis=1, keepdims=True)
+                - normed * jnp.mean(scaled * normed, axis=1, keepdims=True)
+            )
+            work[rows, :] = back
+            low_back = back.astype(BF16)
+            outer_grad[rows, :] = low_back
+            for k, term in enumerate((wide(low_back), given * normed, given)):
+                sums[k] = sums[k] + jnp.sum(term, axis=0, keepdims=True)
+        for k in range(3):
+            vec_grad[9 + k : 10 + k, :] = sums[k]
+        sib_og.start()
+        store_shown.start()
+
+    def inner_back(q):
+        cols = slice(768 * q, 768 * q + 768)
+        resid[...] = dot_nt(outer_grad[...], out[q].reshape(768, 768))
+        total_row = jnp.zeros((1, 768), F32)
+        for r in range(4):
+            rows = pl.ds(128 * r, 128)
+            value = (resid[rows, :] * wide(slope[rows, cols])).astype(BF16)
+            slope[rows, cols] = value
+            total_row = total_row + jnp.sum(wide(value), axis=0, keepdims=True)
+        vec_grad[5 + q : 6 + q, :] = total_row
+        if q == 3:
+            sib_sl.start()
+
+    def put_chunk(j, value):
+        value = value.astype(BF16).reshape(4, 2, 96, 768)
+        if j < 2:
+            grad_out[j] = value
+        else:
+            out[:, :, j - 2] = value
+
+    def chunk_out(j):
+        if j == 0:
+            sib_act.wait_recv()
+            sib_og.wait_recv()
+        mine = active[:, :, pl.ds(2 * at.c + j, 1)].reshape(768, 512)
+        theirs = sib_active[:, :, j].reshape(768, 512)
+        put_chunk(j, dot_nn(mine, outer_grad[...]) + dot_nn(theirs, sib_outer[...]))
+
+    def chunk_in(j):
+        if j == 2:
+            sib_hid.wait_recv()
+            sib_sl.wait_recv()
+        cols = pl.ds(pl.multiple_of(at.c * 1536 + 768 * (j - 2), 128), 768)
+        put_chunk(
+            j,
+            dot_tn(hidden[...], slope[:, cols])
+            + dot_tn(sib_hidden[...], sib_slope[:, 768 * (j - 2) : 768 * (j - 1)]),
+        )
+
+    def chunk_attention(j):
+        if j == 4:
+            sib_tokens.wait_recv()
+            sib_first.wait_recv()
+            value = dot_tn(pair_in[0], stack[at.c]) + dot_tn(sib_in[0], sib_stack[0])
+            put_chunk(j, value * jnp.where(at.c == 0, 0.125, 1.0))
+        else:
+            sib_context.wait_recv()
+            sib_last.wait_recv()
+            put_chunk(j, dot_tn(pair_in[at.c], stack[2 + at.c]) + dot_tn(sib_in[at.c], sib_stack[1]))
+
+    def hidden_back(q):
+        work[...] += dot_nt(slope[:, 768 * q : 768 * q + 768], square(inn.at[q]))
+
+    def middle_norm():
+        sums = [jnp.zeros((1, 768), F32) for _ in range(3)]
+        for r in range(4):
+            rows = pl.ds(128 * r, 128)
+            given = work[rows, :]
+            normed = norm_one[rows, :]
+            scaled = given * vrow(3)
+            back = dev_one[rows, :] * (
+                scaled
+                - jnp.mean(scaled, axis=1, keepdims=True)
+                - normed * jnp.mean(scaled * normed, axis=1, keepdims=True)
+            )
+            work[rows, :] = back
+            low_back = back.astype(BF16)
+            stack[3, rows, :] = low_back
+            for k, term in enumerate((wide(low_back), given * normed, given)):
+                sums[k] = sums[k] + jnp.sum(term, axis=0, keepdims=True)
+        for k in range(3):
+            vec_grad[2 + k : 3 + k, :] = sums[k]
+
+    def context_back():
+        store_shown.wait()
+        shown[...] = dot_nt(stack[3], square(att.at[3])).astype(BF16)
+
+    def attend_back(p):
+        ls_ = pl.ds(128 * p, 128)
+        queries, keys, vals, given = stack[0, :, ls_], stack[2, :, ls_], stack[1, :, ls_], shown[:, ls_]
+        keys_t = keys.T
+        value_grads, key_grads = [], []
+        for h in range(2):
+            mine = jnp.where(low if h == 0 else ~low, vals, jnp.zeros_like(vals))
+            prob_grad = dot_nt(mine, given)
+            weights = probs[2 * p + h]
+            wide_weights = wide(weights)
+            delta = jnp.sum(prob_grad * wide_weights, axis=0, keepdims=True)
+            score_grad = (wide_weights * (prob_grad - delta)).astype(BF16)
+            value_grads.append(dot_nn(weights, given))
+            key_grads.append(dot_nn(score_grad, queries))
+            turn[pl.ds(128 * p + 64 * h, 64), :] = dot_nn(keys_t[64 * h : 64 * h + 64], score_grad).astype(BF16)
+        stack[1, :, ls_] = jnp.where(low, value_grads[0], value_grads[1]).astype(BF16)
+        stack[2, :, ls_] = jnp.where(low, key_grads[0], key_grads[1]).astype(BF16)
+
+    def queries_back():
+        stack[0] = turn[...].T
+        sib_first.start()
+        sib_last.start()
+        vec_grad[0:1, :] = 0.125 * jnp.sum(wide(stack[0]), axis=0, keepdims=True)
+        vec_grad[1:2, :] = jnp.sum(wide(stack[1]), axis=0, keepdims=True)
+
+    def input_back():
+        work[...] += (
+            0.125 * dot_nt(stack[0], square(att.at[0]))
+            + dot_nt(stack[2], square(att.at[1]))
+            + dot_nt(stack[1], square(att.at[2]))
+        )
+        store_grad.start()
+
+    def vec_sum(k):
+        if k == 0:
+            return remote(vec_grad, vec_sib, ws.at[0], wr.at[0], other)
+        if k == 1:
+            return remote(vec_grad, vec_x, ws.at[1], wr.at[1], at.dev(x=1 - at.x))
+        if k == 2:
+            return remote(vec_grad, vec_y, ws.at[2], wr.at[2], at.dev(y=1 - at.y))
+        return remote(vec_z.at[at.z], vec_z.at[at.z], ws.at[k], wr.at[k], at.dev(z=at.far(k - 2)))
+
+    def vec_sum_recv(k):
+        s = lax.rem(at.z + 4 - (k - 2), 4)
+        return remote(vec_z.at[s], vec_z.at[s], ws.at[k], wr.at[k], at.dev(z=at.far(k - 2)))
+
+    def vec_step(k):
+        if k == 0:
+            vec_sum(0).start()
+        elif k <= 2:
+            vec_sum(k - 1).wait()
+            vec_grad[...] += (vec_sib if k == 1 else vec_x)[...]
+            vec_sum(k).start()
+        elif k == 3:
+            vec_sum(2).wait()
+            vec_z[at.z] = vec_grad[...] + vec_y[...]
+            for m in (3, 4, 5):
+                vec_sum(m).start()
+        else:
+            for m in (3, 4, 5):
+                vec_sum_recv(m).wait_recv()
+                vec_sum(m).wait_send()
+            vec_grad[...] = (vec_z[0] + vec_z[1]) + (vec_z[2] + vec_z[3])
+
+    def squares():
+        part = jnp.zeros((96, 768), F32)
+        for b in range(12):
+            value = wide(total[b])
+            part = part + value * value
+        norm_parts[me] = jnp.full((8, 128), jnp.sum(part), F32)
+        for k in range(7):
+            norm_move(k).start()
+        own = jnp.sum(vec_grad[...] * vec_grad[...])
+        for k in range(7):
+            norm_move(k, True).wait_recv()
+        sums = norm_parts[0]
+        for s in range(1, 8):
+            sums = sums + norm_parts[s]
+        norm[...] = sums + own
+
+    def finish():
+        for k in range(7):
+            vec_move(k).wait_send()
+            norm_move(k).wait_send()
+        for cp in (sib_tokens, sib_context, sib_hid, sib_act, sib_og, sib_sl, sib_first, sib_last):
+            cp.wait_send()
+        store_grad.wait()
+        rd.finish()
+
+    run = {
+        "init": init, "early": early, "vec": vectors_here, "qk": queries_keys, "v": values, "wo": project_out,
+        "out": feed_out, "ln2": end_norm, "ln1": middle_norm, "dc": context_back, "dq": queries_back,
+        "ig": input_back, "sq": squares, "fin": finish, "agf": ag.finish,
+    }
+    steps = {
+        "at": attend, "ab": attend_back, "F": feed_in, "D": inner_back, "H": hidden_back, "V": vec_step,
+        "G": lambda j: (chunk_out, chunk_in, chunk_attention)[j // 2](j),
+        "s1": rd.s1, "r1": rd.r1, "s4": rd.s4, "s5": rd.s5, "s6": rd.s6,
+        "zown": ag.zown, "yown": ag.yown, "f": ag.join, "g": ag.have,
+    }
+    for k in range(4):
+        steps[f"p{k}"] = functools.partial(rd.p, dz=k)
+        steps[f"q{k}"] = functools.partial(rd.q, dz=k)
+        steps[f"a{k}"] = functools.partial(ag.arrive, s=k)
+        steps[f"t{k}"] = functools.partial(ag.across, s=k)
+    for name, index in order:
+        if name in run:
+            run[name]()
+        else:
+            steps[name](index)
+
+
+def whole_layer(tokens, cotangent, segments, watt, winn, wout, vectors_low, order, alpha_gather, alpha_scatter):
+    na = max(1, sum(alpha_scatter))
+    nb = max(1, CHUNKS - sum(alpha_scatter))
+    vmem, dma = pltpu.VMEM, pltpu.SemaphoreType.DMA
+    flat = (512, 768)
+    scratch = [
+        vmem((4, 4, 2, 96, 768), BF16), vmem((4, 4, 2, 96, 768), BF16), vmem((4, 2, 4, 96, 768), BF16),
+        vmem(flat, F32), vmem(flat, F32), vmem(flat, F32),
+        vmem((2,) + flat, BF16), vmem((4,) + flat, BF16), vmem(flat, BF16), vmem(flat, BF16), vmem(flat, BF16),
+        vmem((768, 512), BF16), vmem((8, 128), BF16),
+        vmem((4, 2, 4, 96, 512), BF16), vmem((512, 3072), BF16), vmem((12, 512, 512), BF16),
+        vmem((512, 512), F32), vmem((16, 768), F32), vmem((512, 1), F32), vmem((8, 128), F32),
+        vmem((2,) + flat, BF16), vmem(flat, BF16), vmem((4, 2, 2, 96, 512), BF16), vmem(flat, BF16),
+        vmem((512, 1536), BF16), vmem((2,) + flat, BF16),
+        vmem((2, 4, 2, 96, 768), BF16),
+        vmem((na, 4, 2, 96, 384), BF16), vmem((na, 4, 96, 384), BF16), vmem((na, 3, 96, 384), BF16),
+        vmem((nb, 4, 96, 768), BF16), vmem((nb, 3, 96, 768), BF16), vmem((nb, 96, 768), BF16),
+        vmem((8, 16, 128), F32), vmem((16, 768), F32), vmem((16, 768), F32), vmem((16, 768), F32),
+        vmem((4, 16, 768), F32), vmem((8, 8, 128), F32),
+    ]
+    for n in ((BLOCKS, 6), (BLOCKS, 4), (BLOCKS, 8), (BLOCKS,), (CHUNKS, 17), (8,), (7,), (6,), (7,)):
+        scratch += [dma(n), dma(n)]
+    scratch += [dma((13,))]
+    local, far = pl.BlockSpec(memory_space=pltpu.VMEM), pl.BlockSpec(memory_space=pl.ANY)
+    return pl.pallas_call(
+        functools.partial(layer_kernel, order, alpha_gather, alpha_scatter),
+        out_shape=[
+            jax.ShapeDtypeStruct(flat, BF16), jax.ShapeDtypeStruct(flat, F32),
+            jax.ShapeDtypeStruct((12, 96, 768), BF16), jax.ShapeDtypeStruct((16, 768), F32),
+            jax.ShapeDtypeStruct((8, 128), F32),
+        ],
+        in_specs=[far, far, local, far, far, far, local],
+        out_specs=[far, far, local, local, local],
+        scratch_shapes=scratch,
+        compiler_params=pltpu.CompilerParams(
+            collective_id=0, has_side_effects=True, vmem_limit_bytes=63 * 2**20
+        ),
+        name="layer",
+    )(
+        tokens, cotangent, segments.reshape(1, 512), watt, winn, wout, vectors_low
+    )
+
+
+def adam_kernel(
+    act_ref, back_ref, norm_ref, vec_ref, grad_att, grad_inn, grad_out,
+    att_w, att_m, att_v, inn_w, inn_m, inn_v, out_w, out_m, out_v, vec_w, vec_m, vec_v,
+    act_new, back_new, norm_new, att_wn, att_mn, att_vn, inn_wn, inn_mn, inn_vn, out_wn, out_mn, out_vn,
+    vec_wn, vec_mn, vec_vn, vec_gn,
+):
+    act_new[...] = act_ref[...]
+    back_new[...] = back_ref[...]
+    length = jnp.sqrt(norm_ref[0:1, 0:1])
+    factor = CLIP / (length + 1e-06)
+    for grad, old, new in (
+        (grad_att, (att_w, att_m, att_v), (att_wn, att_mn, att_vn)),
+        (grad_inn, (inn_w, inn_m, inn_v), (inn_wn, inn_mn, inn_vn)),
+        (grad_out, (out_w, out_m, out_v), (out_wn, out_mn, out_vn)),
+    ):
+        shape = old[0].shape
+        found = adam_update(
+            *(ref[...].reshape(96, 768) for ref in old), grad[...].reshape(96, 768).astype(F32), factor, RATE_MATRIX
+        )
+        for ref, value in zip(new, found):
+            ref[...] = value.reshape(shape)
+
+    @pl.when(pl.program_id(0) == 0)
+    def _():
+        norm_new[...] = length
+        shard = vec_w.shape[1]
+        own = lax.axis_index("fsdp")
+        grad = jnp.zeros(vec_w.shape, F32)
+        for s in range(8):
+            grad = grad + jnp.where(own == s, vec_ref[:12, shard * s : shard * s + shard], 0.0)
+        found = adam_update(vec_w[...], vec_m[...], vec_v[...], grad, factor, RATE_VECTOR)
+        for ref, value in zip((vec_wn, vec_mn, vec_vn), found):
+            ref[...] = value
+        vec_gn[...] = grad * factor
+
+
+def adam_step(activations, input_grad, norm, vec_grad, total, att, inn, out, vec):
+    def whole(a):
+        return pl.BlockSpec(a.shape, lambda k: (0,) * a.ndim)
+
+    def grads(first):
+        return pl.BlockSpec((1, 96, 768), lambda k: (first + k, 0, 0))
+
+    att_spec = pl.BlockSpec((1, 96, 768), lambda k: (k, 0, 0))
+    inn_spec = pl.BlockSpec((96, 768), lambda k: (0, k))
+    out_spec = pl.BlockSpec((96, 768), lambda k: (k, 0))
+    vec_spec = whole(vec[0])
+    rows = pl.BlockSpec((128, 768), lambda k: (k, 0))
+    one = pl.BlockSpec((1, 1), lambda k: (0, 0))
+    like = [jax.ShapeDtypeStruct(a.shape, F32) for a in (*att, *inn, *out, *vec, vec[0])]
+    return pl.pallas_call(
+        adam_kernel,
+        grid=(4,),
+        out_shape=[
+            jax.ShapeDtypeStruct(activations.shape, BF16), jax.ShapeDtypeStruct(input_grad.shape, F32),
+            jax.ShapeDtypeStruct((1, 1), F32), *like,
+        ],
+        in_specs=[
+            rows, rows,
+            whole(norm), whole(vec_grad), grads(8), grads(4), grads(0),
+            *[att_spec] * 3, *[inn_spec] * 3, *[out_spec] * 3, *[vec_spec] * 3,
+        ],
+        out_specs=[rows, rows, one, *[att_spec] * 3, *[inn_spec] * 3, *[out_spec] * 3, *[vec_spec] * 4],
+        compiler_params=pltpu.CompilerParams(vmem_limit_bytes=63 * 2**20),
+        name="adam",
+    )(activations, input_grad, norm, vec_grad, total, total, total, *att, *inn, *out, *vec)
+
+
+ALPHA_GATHER = (1, 1, 0, 1, 1, 0)
+ALPHA_SCATTER = (0, 1, 0, 1, 0, 1)
+ORDER = (
+    ("init", 0), ("yown", 0), ("zown", 0), ("yown", 1), ("yown", 2), ("zown", 1), ("early", 0), ("t0", 0),
+    ("a0", 0), ("a0", 1), ("zown", 2), ("t0", 1), ("a1", 0), ("zown", 3), ("yown", 3), ("t1", 0), ("a1", 1),
+    ("a0", 2), ("t1", 1), ("t2", 0), ("zown", 4), ("t2", 1), ("a2", 0), ("a2", 1), ("yown", 4), ("a0", 3),
+    ("t3", 0), ("yown", 5), ("t3", 1), ("t0", 3), ("zown", 5), ("a1", 3), ("a1", 2), ("f", 0), ("f", 1),
+    ("g", 0), ("a0", 4), ("a2", 3), ("vec", 0), ("qk", 0), ("t1", 3), ("g", 1), ("t0", 2), ("v", 0),
+    ("a1", 4), ("at", 0), ("t1", 2), ("at", 1), ("t2", 3), ("a2", 2), ("a0", 5), ("t2", 2), ("at", 2),
+    ("t3", 3), ("a2", 4), ("at", 3), ("t3", 2), ("t0", 4), ("f", 2), ("a1", 5), ("at", 4), ("t1", 4),
+    ("f", 3), ("t0", 5), ("at", 5), ("t2", 4), ("wo", 0), ("t3", 4), ("g", 2), ("g", 3), ("a2", 5), ("F", 2),
+    ("F", 3), ("f", 4), ("t1", 5), ("F", 0), ("t2", 5), ("t3", 5), ("f", 5), ("g", 4), ("F", 1), ("g", 5),
+    ("out", 0), ("ln2", 0), ("D", 0), ("G", 0), ("s1", 0), ("r1", 0), ("p2", 0), ("G", 1), ("D", 1),
+    ("p1", 0), ("s1", 1), ("p3", 0), ("D", 2), ("agf", 0), ("q2", 0), ("D", 3), ("r1", 1), ("H", 0), ("H", 1),
+    ("G", 2), ("s1", 2), ("q1", 0), ("H", 2), ("p2", 2), ("G", 3), ("q3", 0), ("H", 3), ("p3", 2), ("r1", 2),
+    ("p3", 1), ("ln1", 0), ("q2", 2), ("dc", 0), ("ab", 0), ("ab", 1), ("s1", 3), ("ab", 2), ("r1", 3),
+    ("p1", 2), ("p1", 1), ("q1", 2), ("p2", 1), ("ab", 3), ("q3", 2), ("p0", 0), ("p0", 2), ("ab", 4),
+    ("p2", 3), ("p0", 1), ("q3", 1), ("ab", 5), ("dq", 0), ("p1", 3), ("p0", 3), ("p3", 3), ("V", 0),
+    ("q2", 1), ("G", 4), ("q2", 3), ("s1", 4), ("q0", 1), ("p3", 4), ("G", 5), ("q1", 3), ("p0", 4),
+    ("s1", 5), ("r1", 5), ("q3", 3), ("p2", 4), ("q1", 1), ("V", 1), ("r1", 4), ("p1", 4), ("p2", 5),
+    ("V", 2), ("q0", 2), ("q0", 3), ("q2", 4), ("p3", 5), ("s4", 2), ("s4", 3), ("V", 3), ("q1", 4),
+    ("q3", 4), ("p1", 5), ("p0", 5), ("ig", 0), ("q3", 5), ("V", 4), ("q0", 0), ("s4", 0), ("s4", 1),
+    ("q0", 4), ("q1", 5), ("q2", 5), ("q0", 5), ("s4", 4), ("s5", 0), ("s6", 0), ("s4", 5), ("s5", 1),
+    ("s5", 2), ("s5", 4), ("s5", 3), ("s6", 1), ("s6", 4), ("s5", 5), ("s6", 5), ("s6", 2), ("s6", 3),
+    ("sq", 0), ("fin", 0),
+)
+
+def plain_body(
     tokens,
     segment_ids,
     cotangent,
@@ -293,6 +1134,50 @@
     )
 
 
+def fused_body(
+    tokens,
+    segment_ids,
+    cotangent,
+    attention_weight,
+    attention_first,
+    attention_second,
+    inner_weight,
+    inner_first,
+    inner_second,
+    outer_weight,
+    outer_first,
+    outer_second,
+    vectors,
+    vector_first,
+    vector_second,
+):
+    _, seq_length, model_width = tokens.shape
+    activations, input_grad, total, vec_grad, norm = whole_layer(
+        tokens.reshape(seq_length, model_width),
+        cotangent.reshape(seq_length, model_width),
+        segment_ids,
+        attention_weight,
+        inner_weight,
+        outer_weight,
+        vectors,
+        ORDER,
+        ALPHA_GATHER,
+        ALPHA_SCATTER,
+    )
+    found = adam_step(
+        activations,
+        input_grad,
+        norm,
+        vec_grad,
+        total,
+        (attention_weight, attention_first, attention_second),
+        (inner_weight, inner_first, inner_second),
+        (outer_weight, outer_first, outer_second),
+        (vectors, vector_first, vector_second),
+    )
+    return (found[0][None], found[1][None], found[2].reshape(()), *found[3:])
+
+
 def solution(mesh):
     placed = (
         P(("dp", "fsdp"), None, None),
@@ -311,8 +1196,9 @@
         P(None, "fsdp"),
         P(None, "fsdp"),
     )
+    fused = mesh.shape["dp"] == 4 and mesh.shape["fsdp"] == 8
     return jax.shard_map(
-        body,
+        fused_body if fused else plain_body,
         mesh=mesh,
         in_specs=placed,
         out_specs=(

time: 875 us -> 179 us (0.20)
  waiting for transfers between devices: 600 us -> 0 us
  Pallas kernels: 0 us -> 175 us
  matrix products: 101 us -> 0 us
  blocking collectives: 59.9 us -> 0 us
  local copies, waits for them, and re-layouts: 47.6 us -> 0 us
  other arithmetic: 34.3 us -> 0 us
  between operations: 20.3 us -> 1.12 us
    unnamed x10 -> x0, waiting for transfers between devices: 203 us -> none
    reduce_scatter x2 -> x0, waiting for transfers between devices: 194 us -> none  [the longest x1 98.5 us: body(): lax.psum_scatter(outer_weight_grad.astype(jnp.bfloat16), 'fsdp', scatter_...]
    pallas_call x0 -> x2, Pallas kernels: none -> 175 us  [the longest x1 163 us: whole_layer(): pl.pallas_call(functools.partial(layer_kernel, order, alpha_gather, alpha...]
    all_gather x3 -> x0, waiting for transfers between devices: 162 us -> none  [the longest x1 60 us: body(): lax.all_gather(shards[2], 'fsdp', axis=0, tiled=True)]
    dot_general x19 -> x0, matrix products: 101 us -> none  [the longest x1 20.8 us: body(): jnp.dot(hidden_low, inner_full, preferred_element_type=jnp.float32)]
    psum x1 -> x0, waiting for transfers between devices: 41.6 us -> none  [body(): lax.psum(shard_grads[0].astype(jnp.bfloat16), 'dp').astype(jnp.float32)]
    all_gather x1 -> x0, blocking collectives: 32.4 us -> none  [body(): lax.all_gather(shards[3], 'fsdp', axis=1, tiled=True)]
    psum x2 -> x0, blocking collectives: 27.5 us -> none  [the longest x1 21.8 us: body(): total_squares = lax.psum(local_squares, 'fsdp')]
  transfers between devices with their start and end apart: 8 -> 0, of which waited for: 8 -> 0; matrix products, arithmetic and copies ran while one was open for 9% -> 0% of each run, Pallas kernels for 0% -> 0%
where the time goes in v2:
time: 179 us; the launch traced here: 176 us
  Pallas kernels  175 us (98%)
    pallas_call x1, Pallas kernels, whole_layer(): pl.pallas_call(functools.partial(layer_kernel, order, alpha_gather, alpha...  163 us
    pallas_call x1, Pallas kernels, adam_step(): pl.pallas_call(adam_kernel, grid=(4,), out_shape=[jax.ShapeDtypeStruct(ac...  12.7 us

profile of v2, /device:TPU:0, one launch (start us, length us, event | category | flops | bytes accessed | tf_op | source)
XLA Modules:
  0.0 176.5 jit_solution(17889398165836981452)
XLA Ops:
  0.6 162.6 %layer.1 = (bf16[512,768]{1,0:T(8,128)(2,1)}, f32[512,768]{1,0:T(8,128)}, bf16[12,96,768]{2,1,0:T(8,128)(2,1)}, f32[16,768]{1,0:T(8,128)}, f32[8,128]{1,0:T(8,128)}) custom-call(bf16[512,768]{1,0:T(8,128)(2,1)} %bitcast.5, bf16[512,768]{1,0:T(8,128)(2,1)} %bitcast.6, s32[1,512]{1,0:T(1,128)} %seg_row.1, f32[4,96,768]{2,1,0:T(8,128)} %att_w.1, ...), custom_call_target="tpu_custom_call" | custom-call | tf_op jit(solution)/shard_map/layer/pallas_call | solution.py:829
  163.3 12.7 %adam.1 = (bf16[512,768]{1,0:T(8,128)(2,1)}, f32[512,768]{1,0:T(8,128)}, f32[1,1]{1,0:T(1,128)}, f32[4,96,768]{2,1,0:T(8,128)}, f32[4,96,768]{2,1,0:T(8,128)}, /...) custom-call(bf16[512,768]{1,0:T(8,128)(2,1)} %get-tuple-element.37.a, ...), custom_call_target="tpu_custom_call" | custom-call | tf_op jit(solution)/shard_map/adam/pallas_call | solution.py:898
